TPU v7x, 32 devices: a whole 2x2x4 slice. The times are simulated.
32 devices in a mesh: gx: 8 (over y, x, core), gy: 4 (over z).
Axes of the slice: x: 2, y: 2, z: 4, core: 2. Of those that a mesh axis runs over, the one named last changes fastest.
Arguments:
- conductance: float32 [16, 64, 512], P(None, 'gx', 'gy'), may hold values from 0.2 to 5
- labels: int32 [16, 64, 512], P(None, 'gx', 'gy'), may hold values from 0 to 2, as said below
- cotangent: float32 [2, 16, 64, 512], P(None, None, 'gx', 'gy')
- saved: float32 [2, 16, 64, 512], P(None, None, 'gx', 'gy'), may hold values from 0 to 1
Outputs:
- adjoint: float32 [2, 16, 64, 512], P(None, None, 'gx', 'gy')
- gradient: float32 [16, 64, 512], P(None, 'gx', 'gy')
Inputs may be any that keep to these rules, and one draw needn't show every extreme that they name: `labels`: 0 marks an unseeded voxel, 1 or 2 the class of a seed.
All inputs are finite; a program needn't handle non-finite values.
Results may differ from a plain program's by a relative error of at most 0.0003.
Values sent between devices are 32-bit elements; how exact they have to be, the bound alone decides.
A program may use at most 64 MiB of HBM per device.

v0:
```python
import jax
import jax.numpy as jnp
from jax import lax
from jax.sharding import PartitionSpec as P

ITERS = 3


prior_strength = 1.0


def extended(x, sides, width):
    for axis, dim in sides:
        size, length = (lax.axis_size(axis), x.shape[dim])
        up = [(i, (i + 1) % size) for i in range(size - 1)]
        down = [(j, i) for i, j in up]
        last = lax.slice_in_dim(x, length - width, length, axis=dim)
        initial = lax.slice_in_dim(x, 0, width, axis=dim)
        before = lax.ppermute(last, axis, up)
        after = lax.ppermute(initial, axis, down)
        x = jnp.concatenate([before, x, after], axis=dim)
    return x


def potentials(labels, saved):
    classes = jnp.arange(1, 3, dtype=jnp.int32)[:, None, None, None]
    tagged = labels[None]
    return jnp.where(tagged == classes, 1.0, jnp.where(tagged > 0, 0.0, saved))


def edge_validity(row_count, col_count, depth):
    row_pos = lax.axis_index("gx") * row_count + jnp.arange(row_count, dtype=jnp.int32)
    col_pos = lax.axis_index("gy") * col_count + jnp.arange(col_count, dtype=jnp.int32)
    depth_pos = jnp.arange(depth, dtype=jnp.int32)
    total_rows = row_count * lax.axis_size("gx")
    total_cols = col_count * lax.axis_size("gy")
    return (
        (row_pos > 0).astype(jnp.float32)[None, :, None],
        (row_pos < total_rows - 1).astype(jnp.float32)[None, :, None],
        (col_pos > 0).astype(jnp.float32)[None, None, :],
        (col_pos < total_cols - 1).astype(jnp.float32)[None, None, :],
        (depth_pos > 0).astype(jnp.float32)[:, None, None],
        (depth_pos < depth - 1).astype(jnp.float32)[:, None, None],
    )


def side_slices(padded):
    return (
        padded[..., :-2, 1:-1],
        padded[..., 2:, 1:-1],
        padded[..., 1:-1, :-2],
        padded[..., 1:-1, 2:],
    )


def depth_neighbours(input_vector):
    depth_axis = input_vector.ndim - 3
    depth = input_vector.shape[depth_axis]
    widths = [(0, 0)] * input_vector.ndim
    widths[depth_axis] = (1, 1)
    padded = jnp.pad(input_vector, widths)
    lower = lax.slice_in_dim(padded, 0, depth, axis=depth_axis)
    upper = lax.slice_in_dim(padded, 2, depth + 2, axis=depth_axis)
    return (lower, upper)


def apply_operator(input_vector, unlabelled_mask, weight_field):
    mask_applied = unlabelled_mask * input_vector
    padded = extended(mask_applied, (("gx", 2), ("gy", 3)), 1)
    neighbours = side_slices(padded) + depth_neighbours(mask_applied)
    graph_laplacian = jnp.zeros_like(mask_applied)
    for weight, neighbour in zip(weight_field, neighbours):
        graph_laplacian = graph_laplacian + weight * (mask_applied - neighbour)
    return (
        unlabelled_mask * (prior_strength * mask_applied + graph_laplacian)
        + (1.0 - unlabelled_mask) * input_vector
    )


def class_sum(first_vec, second_vec):
    return jnp.sum(first_vec * second_vec, axis=(1, 2, 3))


def expand(scalars):
    return scalars[:, None, None, None]


def global_norm(solver_residual):
    return lax.psum(class_sum(solver_residual, solver_residual), ("gx", "gy"))


def per_device(conductance, labels, cotangent, saved):
    depth, row_count, col_count = conductance.shape
    validity = edge_validity(row_count, col_count, depth)
    potential = potentials(labels, saved)
    unlabelled_mask = (labels == 0).astype(jnp.float32)[None]
    solver_residual = unlabelled_mask * cotangent
    cond_pad = extended(conductance, (("gx", 1), ("gy", 2)), 1)
    cond_neighbours = side_slices(cond_pad) + depth_neighbours(conductance)
    weight_field = [
        0.5 * (conductance + neighbour) * valid_edge
        for neighbour, valid_edge in zip(cond_neighbours, validity)
    ]
    adjoint = jnp.zeros_like(solver_residual)
    search_direction = solver_residual
    norm_now = global_norm(solver_residual)
    for iteration in range(ITERS):
        operator_result = apply_operator(search_direction, unlabelled_mask, weight_field)
        step_size = norm_now / lax.psum(class_sum(search_direction, operator_result), ("gx", "gy"))
        adjoint = adjoint + expand(step_size) * search_direction
        solver_residual = solver_residual - expand(step_size) * operator_result
        if iteration + 1 < ITERS:
            norm_next = global_norm(solver_residual)
            search_direction = solver_residual + expand(norm_next / norm_now) * search_direction
            norm_now = norm_next
    joined = extended(jnp.concatenate((adjoint, potential), axis=0), (("gx", 2), ("gy", 3)), 1)
    adj_pad = joined[:2]
    pot_pad = joined[2:]
    adj_neighbours = side_slices(adj_pad) + depth_neighbours(adjoint)
    pot_neighbours = side_slices(pot_pad) + depth_neighbours(potential)
    gradient = jnp.zeros_like(conductance)
    for adj_nb, pot_nb, valid_edge in zip(adj_neighbours, pot_neighbours, validity):
        gradient = (
            gradient - jnp.sum((adjoint - adj_nb) * (potential - pot_nb), axis=0) * valid_edge
        )
    return (adjoint, 0.5 * gradient)


def solution(mesh):
    return jax.shard_map(
        per_device,
        mesh=mesh,
        in_specs=(
            P(None, "gx", "gy"),
            P(None, "gx", "gy"),
            P(None, None, "gx", "gy"),
            P(None, None, "gx", "gy"),
        ),
        out_specs=(P(None, None, "gx", "gy"), P(None, "gx", "gy")),
        check_vma=False,
    )
```

profile of v0, /device:TPU:0, one launch (start us, length us, event | category | flops | bytes accessed | tf_op | source)
XLA Modules:
  0.0 305.2 jit_solution(3853849122864069212)
XLA Ops:
  0.6 0.9 broadcast_compare_fusion
  1.5 0.0 copy-done.1
  1.6 0.0 copy-start.2
  1.6 2.5 collective-permute-start.1
  4.1 1.3 collective-permute-start.3
  5.5 5.1 %collective-permute-start = (f32[16,1,128]{2,1,0:T(1,128)S(1)}, f32[16,1,128]{2,1,0:T(1,128)S(1)}, u32[]{:S(2)}, u32[]{:S(2)}) collective-permute-start(f32[16,1,128]{2,1,0:T(1,128)S(1)} %get-tuple-element.46), channel_id=1, source_target_pairs={{0,4},{4,8},{8,12},{12,16},{16,20},{20,24},{24,28},{1,5},{5,9},{9,... | collective-permute-start | bytes 24584 | tf_op jit(solution)/shard_map/ppermute | solution.py:19
  10.6 1.3 collective-permute-start.2
  12.0 0.1 fusion.83
  12.1 0.0 collective-permute-done
  12.1 2.8 collective-permute-done.2
  14.9 0.1 fusion.102
  15.0 3.5 %collective-permute-start.4 = (f32[16,10,1]{2,1,0:T(8,128)S(1)}, f32[16,10,1]{2,1,0:T(8,128)S(1)}, u32[]{:S(2)}, u32[]{:S(2)}) collective-permute-start(f32[16,10,1]{2,1,0:T(8,128)S(1)} %get-tuple-element.35), channel_id=1, source_target_pairs={{0,1},{1,2},{2,3},{4,5},{5,6},{6,7},{8,9},{9,10},{10,11},{12,13},{... | collective-permute-start | bytes 1928 | tf_op jit(solution)/shard_map/ppermute | solution.py:19
  18.5 1.3 collective-permute-start.6
  19.8 0.0 collective-permute-done.3
  19.9 0.1 pad_maximum_fusion.1
  19.9 0.1 fusion.99
  20.0 4.6 %collective-permute-start.5 = (f32[2,16,10,1]{3,2,1,0:T(8,128)S(1)}, f32[2,16,10,1]{3,2,1,0:T(8,128)S(1)}, u32[]{:S(2)}, u32[]{:S(2)}) collective-permute-start(f32[2,16,10,1]{3,2,1,0:T(8,128)S(1)} %get-tuple-element.29), channel_id=1, source_target_pairs={{0,1},{1,2},{2,3},{4,5},{5,6},{6,7},{8,9},{9,10},{10,11},{12,13},{... | collective-permute-start | bytes 3848 | tf_op jit(solution)/shard_map/ppermute | solution.py:19
  24.6 1.3 collective-permute-start.7
  25.9 0.2 fusion.89
  26.1 4.3 %collective-permute-done.5 = f32[2,16,10,1]{3,2,1,0:T(8,128)S(1)} collective-permute-done((f32[2,16,10,1]{3,2,1,0:T(8,128)S(1)}, f32[2,16,10,1]{3,2,1,0:T(8,128)S(1)}, u32[]{:S(2)}, u32[]{:S(2)}) %collective-permute-start.5) | collective-permute-done | bytes 1312 | tf_op jit(solution)/shard_map/ppermute | solution.py:19
  30.4 4.7 %collective-permute-done.7 = f32[2,16,10,1]{3,2,1,0:T(8,128)S(1)} collective-permute-done((f32[2,16,10,1]{3,2,1,0:T(8,128)S(1)}, f32[2,16,10,1]{3,2,1,0:T(8,128)S(1)}, u32[]{:S(2)}, u32[]{:S(2)}) %collective-permute-start.7) | collective-permute-done | bytes 1312 | tf_op jit(solution)/shard_map/ppermute | solution.py:20
  35.2 0.4 multiply_reduce_fusion.3
  35.5 40.3 %all-reduce.6 = (f32[2]{0:T(128)S(1)}, f32[2]{0:T(128)S(1)}) all-reduce(f32[2]{0:T(128)S(1)} %get-tuple-element.9, f32[2]{0:T(128)S(1)} %get-tuple-element.8), channel_id=1, replica_groups=mesh['gx'=8,'gy'=4] {'gx','gy'}, use_global_device_ids=true, to_apply=%region_1.2 | all-reduce | flops 4 | bytes 32 | tf_op jit(solution)/shard_map/psum | solution.py:89
  75.8 0.2 multiply_reduce_fusion.2
  76.0 40.0 %psum.44 = f32[2]{0:T(128)S(1)} all-reduce(f32[2]{0:T(128)S(1)} %get-tuple-element.18), channel_id=1, replica_groups=mesh['gx'=8,'gy'=4] {'gx','gy'}, use_global_device_ids=true, to_apply=%region_5.6 | all-reduce | flops 2 | bytes 16 | tf_op jit(solution)/shard_map/psum | solution.py:89
  116.0 0.1 broadcast_multiply_fusion.1
  116.2 1.3 collective-permute-start.8
  117.5 1.3 collective-permute-start.9
  118.8 4.3 %collective-permute-done.9 = f32[2,16,1,128]{3,2,1,0:T(1,128)S(1)} collective-permute-done((f32[2,16,1,128]{3,2,1,0:T(1,128)S(1)}, f32[2,16,1,128]{3,2,1,0:T(1,128)S(1)}, u32[]{:S(2)}, u32[]{:S(2)}) %collective-permute-start.9) | collective-permute-done | bytes 16416 | tf_op jit(solution)/shard_map/ppermute | solution.py:20
  123.1 0.1 fusion.98
  123.2 3.7 %collective-permute-start.10 = (f32[2,16,10,1]{3,2,1,0:T(8,128)S(1)}, f32[2,16,10,1]{3,2,1,0:T(8,128)S(1)}, u32[]{:S(2)}, u32[]{:S(2)}) collective-permute-start(f32[2,16,10,1]{3,2,1,0:T(8,128)S(1)} %get-tuple-element.27), channel_id=1, source_target_pairs={{0,1},{1,2},{2,3},{4,5},{5,6},{6,7},{8,9},{9,10},{10,11},{12,13},{... | collective-permute-start | bytes 3848 | tf_op jit(solution)/shard_map/ppermute | solution.py:19
  126.9 1.3 collective-permute-start.11
  128.2 3.8 %collective-permute-done.10 = f32[2,16,10,1]{3,2,1,0:T(8,128)S(1)} collective-permute-done((f32[2,16,10,1]{3,2,1,0:T(8,128)S(1)}, f32[2,16,10,1]{3,2,1,0:T(8,128)S(1)}, u32[]{:S(2)}, u32[]{:S(2)}) %collective-permute-start.10) | collective-permute-done | bytes 1312 | tf_op jit(solution)/shard_map/ppermute | solution.py:19
  132.0 4.7 %collective-permute-done.11 = f32[2,16,10,1]{3,2,1,0:T(8,128)S(1)} collective-permute-done((f32[2,16,10,1]{3,2,1,0:T(8,128)S(1)}, f32[2,16,10,1]{3,2,1,0:T(8,128)S(1)}, u32[]{:S(2)}, u32[]{:S(2)}) %collective-permute-start.11) | collective-permute-done | bytes 1312 | tf_op jit(solution)/shard_map/ppermute | solution.py:20
  136.8 0.3 multiply_reduce_fusion.1
  137.1 40.5 %psum.45 = f32[2]{0:T(128)S(1)} all-reduce(f32[2]{0:T(128)S(1)} %get-tuple-element.14), channel_id=1, replica_groups=mesh['gx'=8,'gy'=4] {'gx','gy'}, use_global_device_ids=true, to_apply=%region_7.8 | all-reduce | flops 2 | bytes 16 | tf_op jit(solution)/shard_map/psum | solution.py:109
  177.6 0.2 multiply_reduce_fusion
  177.8 39.9 %psum.46 = f32[2]{0:T(128)S(1)} all-reduce(f32[2]{0:T(128)S(1)} %multiply_reduce_fusion), channel_id=1, replica_groups=mesh['gx'=8,'gy'=4] {'gx','gy'}, use_global_device_ids=true, to_apply=%region_9.10 | all-reduce | flops 2 | bytes 16 | tf_op jit(solution)/shard_map/psum | solution.py:89
  217.7 0.1 broadcast_multiply_fusion
  217.8 1.3 collective-permute-start.12
  219.1 1.3 collective-permute-start.13
  220.4 0.1 select_select_fusion
  220.5 4.2 %collective-permute-done.13 = f32[2,16,1,128]{3,2,1,0:T(1,128)S(1)} collective-permute-done((f32[2,16,1,128]{3,2,1,0:T(1,128)S(1)}, f32[2,16,1,128]{3,2,1,0:T(1,128)S(1)}, u32[]{:S(2)}, u32[]{:S(2)}) %collective-permute-start.13) | collective-permute-done | bytes 16416 | tf_op jit(solution)/shard_map/ppermute | solution.py:20
  224.8 0.1 fusion.97
  224.9 3.3 %collective-permute-start.14 = (f32[2,16,10,1]{3,2,1,0:T(8,128)S(1)}, f32[2,16,10,1]{3,2,1,0:T(8,128)S(1)}, u32[]{:S(2)}, u32[]{:S(2)}) collective-permute-start(f32[2,16,10,1]{3,2,1,0:T(8,128)S(1)} %get-tuple-element.25), channel_id=1, source_target_pairs={{0,1},{1,2},{2,3},{4,5},{5,6},{6,7},{8,9},{9,10},{10,11},{12,13},{... | collective-permute-start | bytes 3848 | tf_op jit(solution)/shard_map/ppermute | solution.py:19
  228.2 1.3 collective-permute-start.15
  229.5 3.8 %collective-permute-done.14 = f32[2,16,10,1]{3,2,1,0:T(8,128)S(1)} collective-permute-done((f32[2,16,10,1]{3,2,1,0:T(8,128)S(1)}, f32[2,16,10,1]{3,2,1,0:T(8,128)S(1)}, u32[]{:S(2)}, u32[]{:S(2)}) %collective-permute-start.14) | collective-permute-done | bytes 1312 | tf_op jit(solution)/shard_map/ppermute | solution.py:19
  233.3 4.7 %collective-permute-done.15 = f32[2,16,10,1]{3,2,1,0:T(8,128)S(1)} collective-permute-done((f32[2,16,10,1]{3,2,1,0:T(8,128)S(1)}, f32[2,16,10,1]{3,2,1,0:T(8,128)S(1)}, u32[]{:S(2)}, u32[]{:S(2)}) %collective-permute-start.15) | collective-permute-done | bytes 1312 | tf_op jit(solution)/shard_map/ppermute | solution.py:20
  238.0 0.4 fusion.81
  238.4 39.8 %psum.47 = f32[2]{0:T(128)S(1)} all-reduce(f32[2]{0:T(128)S(1)} %fusion.81), channel_id=1, replica_groups=mesh['gx'=8,'gy'=4] {'gx','gy'}, use_global_device_ids=true, to_apply=%region_11.12 | all-reduce | flops 2 | bytes 16 | tf_op jit(solution)/shard_map/psum | solution.py:109
  278.2 0.1 multiply_add_fusion
  278.3 0.0 copy-start
  278.3 1.3 collective-permute-start.16
  279.6 1.3 collective-permute-start.17
  280.9 4.3 %collective-permute-done.17 = f32[4,16,1,128]{3,2,1,0:T(1,128)S(1)} collective-permute-done((f32[4,16,1,128]{3,2,1,0:T(1,128)S(1)}, f32[4,16,1,128]{3,2,1,0:T(1,128)S(1)}, u32[]{:S(2)}, u32[]{:S(2)}) %collective-permute-start.17) | collective-permute-done | bytes 32800 | tf_op jit(solution)/shard_map/ppermute | solution.py:20
  285.2 0.1 pad_maximum_fusion
  285.3 0.2 fusion.96
  285.5 3.3 %collective-permute-start.18 = (f32[4,16,10,1]{3,2,1,0:T(8,128)S(1)}, f32[4,16,10,1]{3,2,1,0:T(8,128)S(1)}, u32[]{:S(2)}, u32[]{:S(2)}) collective-permute-start(f32[4,16,10,1]{3,2,1,0:T(8,128)S(1)} %get-tuple-element.21), channel_id=1, source_target_pairs={{0,1},{1,2},{2,3},{4,5},{5,6},{6,7},{8,9},{9,10},{10,11},{12,13},{... | collective-permute-start | bytes 7688 | tf_op jit(solution)/shard_map/ppermute | solution.py:19
  288.9 1.3 collective-permute-start.19
  290.2 9.2 %collective-permute-done.18 = f32[4,16,10,1]{3,2,1,0:T(8,128)S(1)} collective-permute-done((f32[4,16,10,1]{3,2,1,0:T(8,128)S(1)}, f32[4,16,10,1]{3,2,1,0:T(8,128)S(1)}, u32[]{:S(2)}, u32[]{:S(2)}) %collective-permute-start.18) | collective-permute-done | bytes 2592 | tf_op jit(solution)/shard_map/ppermute | solution.py:19
  299.4 0.2 fusion.44
  299.6 4.6 %collective-permute-done.19 = f32[4,16,10,1]{3,2,1,0:T(8,128)S(1)} collective-permute-done((f32[4,16,10,1]{3,2,1,0:T(8,128)S(1)}, f32[4,16,10,1]{3,2,1,0:T(8,128)S(1)}, u32[]{:S(2)}, u32[]{:S(2)}) %collective-permute-start.19) | collective-permute-done | bytes 2592 | tf_op jit(solution)/shard_map/ppermute | solution.py:20
  304.2 0.3 fusion.47
  304.4 0.7 subtract_multiply_fusion
  (36 shorter events, 0.4 us)
Async XLA Ops:
  0.6 0.9 copy-start.1
  1.6 10.4 %copy-start.3 = (s32[16,8,128]{2,1,0:T(8,128)S(1)}, s32[16,8,128]{2,1,0:T(8,128)}, u32[]{:S(2)}) copy-start(s32[16,8,128]{2,1,0:T(8,128)} %param.5) | copy-start | bytes 196612
  1.6 3.8 %copy-start.2 = (f32[16,8,128]{2,1,0:T(8,128)S(1)}, f32[16,8,128]{2,1,0:T(8,128)}, u32[]{:S(2)}) copy-start(f32[16,8,128]{2,1,0:T(8,128)} %param.4) | copy-start | bytes 196612
  1.6 18.2 %collective-permute-start.1 = (f32[2,16,1,128]{3,2,1,0:T(1,128)S(1)}, f32[2,16,1,128]{3,2,1,0:T(1,128)S(1)}, u32[]{:S(2)}, u32[]{:S(2)}) collective-permute-start(f32[2,16,1,128]{3,2,1,0:T(1,128)S(1)} %get-tuple-element.37), channel_id=1, source_target_pairs={{0,4},{4,8},{8,12},{12,16},{16,20},{20,24},{24,28},{1,5},{5,9},{9,... | collective-permute-start | bytes 49160 | tf_op jit(solution)/shard_map/ppermute | solution.py:19
  4.1 15.7 %collective-permute-start.3 = (f32[2,16,1,128]{3,2,1,0:T(1,128)S(1)}, f32[2,16,1,128]{3,2,1,0:T(1,128)S(1)}, u32[]{:S(2)}, u32[]{:S(2)}) collective-permute-start(f32[2,16,1,128]{3,2,1,0:T(1,128)S(1)} %get-tuple-element.38), channel_id=1, source_target_pairs={{4,0},{8,4},{12,8},{16,12},{20,16},{24,20},{28,24},{5,1},{9,5},{13... | collective-permute-start | bytes 49160 | tf_op jit(solution)/shard_map/ppermute | solution.py:20
  5.5 6.6 %collective-permute-start = (f32[16,1,128]{2,1,0:T(1,128)S(1)}, f32[16,1,128]{2,1,0:T(1,128)S(1)}, u32[]{:S(2)}, u32[]{:S(2)}) collective-permute-start(f32[16,1,128]{2,1,0:T(1,128)S(1)} %get-tuple-element.46), channel_id=1, source_target_pairs={{0,4},{4,8},{8,12},{12,16},{16,20},{20,24},{24,28},{1,5},{5,9},{9,... | collective-permute-start | bytes 24584 | tf_op jit(solution)/shard_map/ppermute | solution.py:19
  10.6 4.3 %collective-permute-start.2 = (f32[16,1,128]{2,1,0:T(1,128)S(1)}, f32[16,1,128]{2,1,0:T(1,128)S(1)}, u32[]{:S(2)}, u32[]{:S(2)}) collective-permute-start(f32[16,1,128]{2,1,0:T(1,128)S(1)} %get-tuple-element.47), channel_id=1, source_target_pairs={{4,0},{8,4},{12,8},{16,12},{20,16},{24,20},{28,24},{5,1},{9,5},{13... | collective-permute-start | bytes 24584 | tf_op jit(solution)/shard_map/ppermute | solution.py:20
  15.0 10.9 %collective-permute-start.4 = (f32[16,10,1]{2,1,0:T(8,128)S(1)}, f32[16,10,1]{2,1,0:T(8,128)S(1)}, u32[]{:S(2)}, u32[]{:S(2)}) collective-permute-start(f32[16,10,1]{2,1,0:T(8,128)S(1)} %get-tuple-element.35), channel_id=1, source_target_pairs={{0,1},{1,2},{2,3},{4,5},{5,6},{6,7},{8,9},{9,10},{10,11},{12,13},{... | collective-permute-start | bytes 1928 | tf_op jit(solution)/shard_map/ppermute | solution.py:19
  18.5 7.4 %collective-permute-start.6 = (f32[16,10,1]{2,1,0:T(8,128)S(1)}, f32[16,10,1]{2,1,0:T(8,128)S(1)}, u32[]{:S(2)}, u32[]{:S(2)}) collective-permute-start(f32[16,10,1]{2,1,0:T(8,128)S(1)} %get-tuple-element.36), channel_id=1, source_target_pairs={{1,0},{2,1},{3,2},{5,4},{6,5},{7,6},{9,8},{10,9},{11,10},{13,12},{... | collective-permute-start | bytes 1928 | tf_op jit(solution)/shard_map/ppermute | solution.py:20
  20.0 10.4 %collective-permute-start.5 = (f32[2,16,10,1]{3,2,1,0:T(8,128)S(1)}, f32[2,16,10,1]{3,2,1,0:T(8,128)S(1)}, u32[]{:S(2)}, u32[]{:S(2)}) collective-permute-start(f32[2,16,10,1]{3,2,1,0:T(8,128)S(1)} %get-tuple-element.29), channel_id=1, source_target_pairs={{0,1},{1,2},{2,3},{4,5},{5,6},{6,7},{8,9},{9,10},{10,11},{12,13},{... | collective-permute-start | bytes 3848 | tf_op jit(solution)/shard_map/ppermute | solution.py:19
  24.6 10.5 %collective-permute-start.7 = (f32[2,16,10,1]{3,2,1,0:T(8,128)S(1)}, f32[2,16,10,1]{3,2,1,0:T(8,128)S(1)}, u32[]{:S(2)}, u32[]{:S(2)}) collective-permute-start(f32[2,16,10,1]{3,2,1,0:T(8,128)S(1)} %get-tuple-element.30), channel_id=1, source_target_pairs={{1,0},{2,1},{3,2},{5,4},{6,5},{7,6},{9,8},{10,9},{11,10},{13,12},{... | collective-permute-start | bytes 3848 | tf_op jit(solution)/shard_map/ppermute | solution.py:20
  116.2 2.6 collective-permute-start.8
  117.5 5.6 %collective-permute-start.9 = (f32[2,16,1,128]{3,2,1,0:T(1,128)S(1)}, f32[2,16,1,128]{3,2,1,0:T(1,128)S(1)}, u32[]{:S(2)}, u32[]{:S(2)}) collective-permute-start(f32[2,16,1,128]{3,2,1,0:T(1,128)S(1)} %get-tuple-element.34), channel_id=1, source_target_pairs={{4,0},{8,4},{12,8},{16,12},{20,16},{24,20},{28,24},{5,1},{9,5},{13... | collective-permute-start | bytes 49160 | tf_op jit(solution)/shard_map/ppermute | solution.py:20
  123.2 8.8 %collective-permute-start.10 = (f32[2,16,10,1]{3,2,1,0:T(8,128)S(1)}, f32[2,16,10,1]{3,2,1,0:T(8,128)S(1)}, u32[]{:S(2)}, u32[]{:S(2)}) collective-permute-start(f32[2,16,10,1]{3,2,1,0:T(8,128)S(1)} %get-tuple-element.27), channel_id=1, source_target_pairs={{0,1},{1,2},{2,3},{4,5},{5,6},{6,7},{8,9},{9,10},{10,11},{12,13},{... | collective-permute-start | bytes 3848 | tf_op jit(solution)/shard_map/ppermute | solution.py:19
  126.9 9.8 %collective-permute-start.11 = (f32[2,16,10,1]{3,2,1,0:T(8,128)S(1)}, f32[2,16,10,1]{3,2,1,0:T(8,128)S(1)}, u32[]{:S(2)}, u32[]{:S(2)}) collective-permute-start(f32[2,16,10,1]{3,2,1,0:T(8,128)S(1)} %get-tuple-element.28), channel_id=1, source_target_pairs={{1,0},{2,1},{3,2},{5,4},{6,5},{7,6},{9,8},{10,9},{11,10},{13,12},{... | collective-permute-start | bytes 3848 | tf_op jit(solution)/shard_map/ppermute | solution.py:20
  217.7 2.7 copy-start.4
  217.8 2.7 collective-permute-start.12
  219.1 5.6 %collective-permute-start.13 = (f32[2,16,1,128]{3,2,1,0:T(1,128)S(1)}, f32[2,16,1,128]{3,2,1,0:T(1,128)S(1)}, u32[]{:S(2)}, u32[]{:S(2)}) collective-permute-start(f32[2,16,1,128]{3,2,1,0:T(1,128)S(1)} %get-tuple-element.32), channel_id=1, source_target_pairs={{4,0},{8,4},{12,8},{16,12},{20,16},{24,20},{28,24},{5,1},{9,5},{13... | collective-permute-start | bytes 49160 | tf_op jit(solution)/shard_map/ppermute | solution.py:20
  224.9 8.4 %collective-permute-start.14 = (f32[2,16,10,1]{3,2,1,0:T(8,128)S(1)}, f32[2,16,10,1]{3,2,1,0:T(8,128)S(1)}, u32[]{:S(2)}, u32[]{:S(2)}) collective-permute-start(f32[2,16,10,1]{3,2,1,0:T(8,128)S(1)} %get-tuple-element.25), channel_id=1, source_target_pairs={{0,1},{1,2},{2,3},{4,5},{5,6},{6,7},{8,9},{9,10},{10,11},{12,13},{... | collective-permute-start | bytes 3848 | tf_op jit(solution)/shard_map/ppermute | solution.py:19
  228.2 9.8 %collective-permute-start.15 = (f32[2,16,10,1]{3,2,1,0:T(8,128)S(1)}, f32[2,16,10,1]{3,2,1,0:T(8,128)S(1)}, u32[]{:S(2)}, u32[]{:S(2)}) collective-permute-start(f32[2,16,10,1]{3,2,1,0:T(8,128)S(1)} %get-tuple-element.26), channel_id=1, source_target_pairs={{1,0},{2,1},{3,2},{5,4},{6,5},{7,6},{9,8},{10,9},{11,10},{13,12},{... | collective-permute-start | bytes 3848 | tf_op jit(solution)/shard_map/ppermute | solution.py:20
  278.3 25.9 %copy-start = (f32[2,16,8,128]{3,2,1,0:T(8,128)}, f32[2,16,8,128]{3,2,1,0:T(8,128)S(1)}, u32[]{:S(2)}) copy-start(f32[2,16,8,128]{3,2,1,0:T(8,128)S(1)} %multiply_add_fusion) | copy-start | bytes 393220
  278.3 2.6 collective-permute-start.16
  279.6 5.6 %collective-permute-start.17 = (f32[4,16,1,128]{3,2,1,0:T(1,128)S(1)}, f32[4,16,1,128]{3,2,1,0:T(1,128)S(1)}, u32[]{:S(2)}, u32[]{:S(2)}) collective-permute-start(f32[4,16,1,128]{3,2,1,0:T(1,128)S(1)} %get-tuple-element.23), channel_id=1, source_target_pairs={{4,0},{8,4},{12,8},{16,12},{20,16},{24,20},{28,24},{5,1},{9,5},{13... | collective-permute-start | bytes 98312 | tf_op jit(solution)/shard_map/ppermute | solution.py:20
  285.5 13.9 %collective-permute-start.18 = (f32[4,16,10,1]{3,2,1,0:T(8,128)S(1)}, f32[4,16,10,1]{3,2,1,0:T(8,128)S(1)}, u32[]{:S(2)}, u32[]{:S(2)}) collective-permute-start(f32[4,16,10,1]{3,2,1,0:T(8,128)S(1)} %get-tuple-element.21), channel_id=1, source_target_pairs={{0,1},{1,2},{2,3},{4,5},{5,6},{6,7},{8,9},{9,10},{10,11},{12,13},{... | collective-permute-start | bytes 7688 | tf_op jit(solution)/shard_map/ppermute | solution.py:19
  288.9 15.3 %collective-permute-start.19 = (f32[4,16,10,1]{3,2,1,0:T(8,128)S(1)}, f32[4,16,10,1]{3,2,1,0:T(8,128)S(1)}, u32[]{:S(2)}, u32[]{:S(2)}) collective-permute-start(f32[4,16,10,1]{3,2,1,0:T(8,128)S(1)} %get-tuple-element.22), channel_id=1, source_target_pairs={{1,0},{2,1},{3,2},{5,4},{6,5},{7,6},{9,8},{10,9},{11,10},{13,12},{... | collective-permute-start | bytes 7688 | tf_op jit(solution)/shard_map/ppermute | solution.py:20
where the time goes:
time: 308 us; the launch traced here: 305 us
  blocking collectives  200 us (65%)
  waiting for transfers between devices  55.4 us (18%)
  starting transfers between devices  42.8 us (14%)
  other arithmetic  4.61 us (1%)
    psum x3, blocking collectives, global_norm(): return lax.psum(class_sum(solver_residual, solver_residual), ('gx', 'gy'))  120 us
    psum x2, blocking collectives, per_device(): lax.psum(class_sum(search_direction, operator_result), ('gx', 'gy'))  80.2 us
    ppermute x10, waiting for transfers between devices, extended(): after = lax.ppermute(initial, axis, down)  34.3 us
    ppermute x10, starting transfers between devices, extended(): before = lax.ppermute(last, axis, up)  29.8 us
    ppermute x10, waiting for transfers between devices, extended(): before = lax.ppermute(last, axis, up)  21.1 us
    ppermute x10, starting transfers between devices, extended(): after = lax.ppermute(initial, axis, down)  12.9 us
  transfers between devices with their start and end apart: 20, of which 12 were waited for; matrix products, arithmetic and copies ran while one was open for 0% of the time, Pallas kernels for 0%

commit v1 on v0

v1 whole, which is shorter than its diff:
```python
import jax
import jax.numpy as jnp
from jax import lax
from jax.experimental import pallas as pl
from jax.experimental.pallas import tpu as pltpu
from jax.sharding import PartitionSpec as P

SHIFT = 2.0
SCALE = 32.0
HALO = 3
MESH = pl.DeviceIdType.MESH


def kernel(
    n_gx, n_gy,
    cond_ref, label_ref, cot_ref, saved_ref,
    adj_ref, grad_ref,
    ce, me, pe, v0, v1, v2, wx, wy, wz, dd, gk,
    xsend, xrecv, ysend, yrecv, pay, slots_x, mid, slots_y,
    send_sem, recv_sem, gx_send, gx_recv, gy_send, gy_recv,
):
    depth, rows, cols = cond_ref.shape
    R2, C2 = 2 * rows, 2 * cols
    gx = lax.axis_index("gx")
    gy = lax.axis_index("gy")
    has_up, has_down = gx > 0, gx < n_gx - 1
    has_left, has_right = gy > 0, gy < n_gy - 1

    sides = [(-1, 0), (1, 0), (0, -1), (0, 1), (-1, -1), (-1, 1), (1, -1), (1, 1)]

    def exists(dx, dy):
        ok = None
        for d, low, high in ((dx, has_up, has_down), (dy, has_left, has_right)):
            if d:
                here = low if d < 0 else high
                ok = here if ok is None else jnp.logical_and(ok, here)
        return ok

    barrier = pltpu.get_barrier_semaphore()
    for o in range(1, n_gx):
        pl.semaphore_signal(barrier, inc=1, device_id=(lax.rem(gx + o, n_gx), gy), device_id_type=MESH)
    for o in range(1, n_gy):
        pl.semaphore_signal(barrier, inc=1, device_id=(gx, lax.rem(gy + o, n_gy)), device_id_type=MESH)
    for dx, dy in sides[4:]:
        @pl.when(exists(dx, dy))
        def _():
            pl.semaphore_signal(barrier, inc=1, device_id=(gx + dx, gy + dy), device_id_type=MESH)

    lane = lax.broadcasted_iota(jnp.int32, (rows, cols), 1)
    slot_lanes = cols // depth
    packs = [jnp.zeros((rows, cols), jnp.float32) for _ in range(6)]
    zero_tile = jnp.zeros((rows, cols), jnp.float32)
    for z in range(depth):
        lab = label_ref[z]
        m = jnp.where(lab == 0, 1.0, 0.0)
        fields = [m * cot_ref[0, z], m * cot_ref[1, z], cond_ref[z], m]
        for k in range(2):
            fields.append(jnp.where(lab == k + 1, 1.0, jnp.where(lab > 0, 0.0, saved_ref[k, z])))
        v0[0, z + 1, 0:rows, 0:cols] = fields[0]
        v0[1, z + 1, 0:rows, 0:cols] = fields[1]
        ce[z, 0:rows, 0:cols] = fields[2]
        me[z, 0:rows, 0:cols] = m
        pe[0, z, 0:rows, 0:cols] = fields[4]
        pe[1, z, 0:rows, 0:cols] = fields[5]
        at = 0
        for f, width in zip(fields, (3, 3, 3, 2, 1, 1)):
            first = at + z * width
            xsend[0, first:first + width, :] = f[0:width]
            xsend[1, first:first + width, :] = f[rows - width:rows]
            at += depth * width
        window = lax.rem(lane - z * slot_lanes + HALO + cols, cols) < 2 * HALO
        for i, f in enumerate(fields):
            rolled = pltpu.roll(f, z * slot_lanes, 1) if z else f
            packs[i] = jnp.where(window, rolled, packs[i])
    for i in range(6):
        ysend[i] = packs[i]

    partners = n_gx - 1 + n_gy - 1
    for dx, dy in sides[4:]:
        partners = partners + jnp.where(exists(dx, dy), 1, 0)
    pl.semaphore_wait(barrier, partners)

    def halo_copy(i):
        dx, dy = sides[i]
        back = sides.index((-dx, -dy))
        if dy == 0:
            src, dst = xsend.at[0 if dx < 0 else 1], xrecv.at[back]
        else:
            src, dst = ysend, yrecv.at[back - 2]
        return pltpu.make_async_remote_copy(
            src_ref=src, dst_ref=dst, send_sem=send_sem.at[i], recv_sem=recv_sem.at[back],
            device_id=(gx + dx, gy + dy), device_id_type=MESH,
        )

    def arrival(i):
        dst = xrecv.at[i] if i < 2 else yrecv.at[i - 2]
        return pltpu.make_async_remote_copy(
            src_ref=dst, dst_ref=dst, send_sem=send_sem.at[i], recv_sem=recv_sem.at[i],
            device_id=(gx + sides[i][0], gy + sides[i][1]), device_id_type=MESH,
        )

    for i, (dx, dy) in enumerate(sides):
        @pl.when(exists(dx, dy))
        def _():
            halo_copy(i).start()

        @pl.when(jnp.logical_not(exists(dx, dy)))
        def _():
            if i < 2:
                xrecv[i] = jnp.zeros(xrecv.shape[1:], jnp.float32)
            else:
                yrecv[i - 2] = jnp.zeros(yrecv.shape[1:], jnp.float32)

    edge = jnp.zeros((R2, C2), jnp.float32)
    for v in (v0, v1, v2):
        for k in range(2):
            v[k, 0] = edge
            v[k, depth + 1] = edge
    wz[0] = edge
    for z in range(depth):
        for ref in (v0.at[0, z + 1], v0.at[1, z + 1], ce.at[z], me.at[z], pe.at[0, z], pe.at[1, z]):
            ref[rows:R2, 0:cols] = zero_tile

    for i, (dx, dy) in enumerate(sides):
        @pl.when(exists(dx, dy))
        def _():
            arrival(i).wait_recv()

    row = lax.broadcasted_iota(jnp.int32, (rows, cols), 0)
    after = lax.rem(lane, slot_lanes) < HALO
    beside, corner = [], []
    for i in range(6):
        beside.append(jnp.where(after, yrecv[1, i], yrecv[0, i]))
        if i < 4:
            above = jnp.where(after, yrecv[3, i], yrecv[2, i])
            below = jnp.where(after, yrecv[5, i], yrecv[4, i])
            corner.append(jnp.where(row < rows // 2, below, above))
    window = jnp.logical_or(lane < HALO, lane >= cols - HALO)
    corner_rows = jnp.logical_or(row < HALO, row >= rows - HALO)
    window_corner = jnp.logical_and(window, corner_rows)
    for z in range(depth):
        targets = [v0.at[0, z + 1], v0.at[1, z + 1], ce.at[z], me.at[z], pe.at[0, z], pe.at[1, z]]
        at = 0
        for f, (ref, width) in enumerate(zip(targets, (3, 3, 3, 2, 1, 1))):
            first = at + z * width
            ref[rows:rows + width, 0:cols] = xrecv[1, first:first + width, :]
            ref[R2 - width:R2, 0:cols] = xrecv[0, first:first + width, :]
            at += depth * width
            back = (cols - z * slot_lanes) % cols
            tile = pltpu.roll(beside[f], back, 1) if back else beside[f]
            ref[0:rows, cols:C2] = jnp.where(window, tile, 0.0)
            if f < 4:
                tile = pltpu.roll(corner[f], back, 1) if back else corner[f]
                ref[rows:R2, cols:C2] = jnp.where(window_corner, tile, 0.0)

    big_row = lax.broadcasted_iota(jnp.int32, (R2, C2), 0)
    big_lane = lax.broadcasted_iota(jnp.int32, (R2, C2), 1)
    no_x = jnp.logical_or(
        jnp.logical_and(big_row == rows - 1, jnp.logical_not(has_down)),
        jnp.logical_and(big_row == R2 - 1, jnp.logical_not(has_up)),
    )
    no_y = jnp.logical_or(
        jnp.logical_and(big_lane == cols - 1, jnp.logical_not(has_right)),
        jnp.logical_and(big_lane == C2 - 1, jnp.logical_not(has_left)),
    )
    valid_x = jnp.where(no_x, 0.0, 1.0)
    valid_y = jnp.where(no_y, 0.0, 1.0)
    half_x = valid_x * (0.5 / SCALE)
    half_y = valid_y * (0.5 / SCALE)
    last = depth - 1

    def next_row(a):
        return pltpu.roll(a, a.shape[0] - 1, 0)

    def next_lane(a):
        return pltpu.roll(a, a.shape[1] - 1, 1)

    def weights(z, carry):
        c = ce[z]
        ex = half_x * (c + next_row(c))
        ey = half_y * (c + next_lane(c))
        cn = ce[jnp.minimum(z + 1, last)]
        ez = jnp.where(z < last, 0.5 / SCALE, 0.0) * (c + cn)
        wx[z] = ex
        wy[z] = ey
        wz[z + 1] = ez
        deg = ex + pltpu.roll(ex, 1, 0) + ey + pltpu.roll(ey, 1, 1) + ez + wz[z]
        dd[z] = deg + (1.0 - SHIFT) / SCALE
        return carry

    lax.fori_loop(0, depth, weights, 0, unroll=2)

    def apply_full(src, dst, sums):
        def body(z, carry):
            ex, ey, ez, ezm, d, m = wx[z], wy[z], wz[z + 1], wz[z], dd[z], me[z]
            out = []
            for k in range(2):
                v = src[k, z + 1]
                a = d * v - ez * src[k, z + 2] - ezm * src[k, z]
                a = a - ex * next_row(v) - pltpu.roll(ex * v, 1, 0)
                a = a - ey * next_lane(v) - pltpu.roll(ey * v, 1, 1)
                a = m * a
                dst[k, z + 1] = a
                old, new = v[0:rows, 0:cols], a[0:rows, 0:cols]
                out.append(carry[3 * k] + old * old)
                out.append(carry[3 * k + 1] + old * new)
                out.append(carry[3 * k + 2] + new * new)
            return tuple(out)
        return lax.fori_loop(0, depth, body, (zero_tile,) * 6, unroll=2)

    first = apply_full(v0, v1, True)
    second = apply_full(v1, v2, True)

    def apply_core(z, carry):
        exr = wx[z, :, 0:cols]
        eyr = wy[z, 0:rows, :]
        ez, ezm = wz[z + 1, 0:rows, 0:cols], wz[z, 0:rows, 0:cols]
        d, m = dd[z, 0:rows, 0:cols], me[z, 0:rows, 0:cols]
        out = []
        for k in range(2):
            vx = v2[k, z + 1, :, 0:cols]
            vy = v2[k, z + 1, 0:rows, :]
            v = vx[0:rows]
            a = d * v - ez * v2[k, z + 2, 0:rows, 0:cols] - ezm * v2[k, z, 0:rows, 0:cols]
            a = a - (exr * next_row(vx) + pltpu.roll(exr * vx, 1, 0))[0:rows]
            a = a - (eyr * next_lane(vy) + pltpu.roll(eyr * vy, 1, 1))[:, 0:cols]
            out.append(carry[k] + v * (m * a))
        return tuple(out)

    third = lax.fori_loop(0, depth, apply_core, (zero_tile,) * 2, unroll=2)

    for k in range(2):
        moments = [first[3 * k], first[3 * k + 1], first[3 * k + 2],
                   second[3 * k + 1], second[3 * k + 2], third[k]]
        for j, a in enumerate(moments):
            pay[8 * k + j:8 * k + j + 1, :] = jnp.sum(a, axis=0, keepdims=True)
        pay[8 * k + 6:8 * k + 8, :] = jnp.zeros((2, cols), jnp.float32)

    def gx_copy(o):
        return pltpu.make_async_remote_copy(
            src_ref=pay, dst_ref=slots_x.at[gx], send_sem=gx_send.at[o], recv_sem=gx_recv.at[o],
            device_id=(lax.rem(gx + o, n_gx), gy), device_id_type=MESH,
        )

    def gy_copy(o):
        return pltpu.make_async_remote_copy(
            src_ref=mid, dst_ref=slots_y.at[gy], send_sem=gy_send.at[o], recv_sem=gy_recv.at[o],
            device_id=(gx, lax.rem(gy + o, n_gy)), device_id_type=MESH,
        )

    for o in range(1, n_gx):
        gx_copy(o).start()
    slots_x[gx] = pay[...]

    vx_edge = valid_x[:, 0:cols]
    vy_edge = valid_y[0:rows, :]

    def parts(k):
        def body(z, carry):
            up = jnp.minimum(z + 1, last)
            down = jnp.maximum(z - 1, 0)
            px = pe[k, z, :, 0:cols]
            py = pe[k, z, 0:rows, :]
            p = px[0:rows]
            dx = vx_edge * (px - next_row(px))
            dy = vy_edge * (py - next_lane(py))
            du = p - pe[k, up, 0:rows, 0:cols]
            dn = p - pe[k, down, 0:rows, 0:cols]
            for j, v in enumerate((v0, v1, v2)):
                ax = v[k, z + 1, :, 0:cols]
                ay = v[k, z + 1, 0:rows, :]
                a = ax[0:rows]
                qx = dx * (ax - next_row(ax))
                qy = dy * (ay - next_lane(ay))
                g = qx[0:rows] + pltpu.roll(qx, 1, 0)[0:rows]
                g = g + qy[:, 0:cols] + pltpu.roll(qy, 1, 1)[:, 0:cols]
                g = g + du * (a - v[k, z + 2, 0:rows, 0:cols])
                g = g + dn * (a - v[k, z, 0:rows, 0:cols])
                gk[3 * k + j, z] = g
            return carry
        lax.fori_loop(0, depth, body, 0, unroll=2)

    parts(0)
    for o in range(1, n_gx):
        gx_copy(o).wait_recv()
    total = slots_x[0]
    for i in range(1, n_gx):
        total = total + slots_x[i]
    mid[...] = total
    for o in range(1, n_gy):
        gy_copy(o).start()
    slots_y[gy] = total
    parts(1)
    for o in range(1, n_gy):
        gy_copy(o).wait_recv()
    total = slots_y[0]
    for i in range(1, n_gy):
        total = total + slots_y[i]
    total = jnp.broadcast_to(jnp.sum(total, axis=1, keepdims=True), total.shape)

    coeffs = []
    for k in range(2):
        m = [total[8 * k + j:8 * k + j + 1, :] for j in range(6)]
        h = [SCALE * m[j + 1] + SHIFT * m[j] for j in range(5)]
        l1, l2 = h[1] / h[0], h[2] / h[0]
        a11, a12, a22 = h[2] - l1 * h[1], h[3] - l1 * h[2], h[4] - l2 * h[2]
        b1, b2 = m[1] - l1 * m[0], m[2] - l2 * m[0]
        l3 = a12 / a11
        c2 = (b2 - l3 * b1) / (a22 - l3 * a12)
        c1 = (b1 - a12 * c2) / a11
        c0 = (m[0] - h[1] * c1 - h[2] * c2) / h[0]
        coeffs.append([jnp.broadcast_to(c, (rows, cols)) for c in (c0, c1, c2)])

    for z in range(depth):
        grad = zero_tile
        for k in range(2):
            acc = zero_tile
            for j, v in enumerate((v0, v1, v2)):
                acc = acc + coeffs[k][j] * v[k, z + 1, 0:rows, 0:cols]
                grad = grad + coeffs[k][j] * gk[3 * k + j, z]
            adj_ref[k, z] = acc
        grad_ref[z] = -0.5 * grad

    for i, (dx, dy) in enumerate(sides):
        @pl.when(exists(dx, dy))
        def _():
            halo_copy(i).wait_send()
    for o in range(1, n_gx):
        gx_copy(o).wait_send()
    for o in range(1, n_gy):
        gy_copy(o).wait_send()


def solution(mesh):
    n_gx, n_gy = mesh.shape["gx"], mesh.shape["gy"]

    def per_device(conductance, labels, cotangent, saved):
        depth, rows, cols = conductance.shape
        f32 = jnp.float32
        big = (depth, 2 * rows, 2 * cols)
        padded = (2, depth + 2, 2 * rows, 2 * cols)
        face = depth * 13
        vmem = pl.BlockSpec(memory_space=pltpu.VMEM)
        dma = pltpu.SemaphoreType.DMA
        return pl.pallas_call(
            lambda *refs: kernel(n_gx, n_gy, *refs),
            out_shape=(
                jax.ShapeDtypeStruct(cotangent.shape, f32),
                jax.ShapeDtypeStruct(conductance.shape, f32),
            ),
            in_specs=[vmem] * 4,
            out_specs=(vmem, vmem),
            scratch_shapes=[
                pltpu.VMEM(big, f32),
                pltpu.VMEM(big, f32),
                pltpu.VMEM((2,) + big, f32),
                pltpu.VMEM(padded, f32),
                pltpu.VMEM(padded, f32),
                pltpu.VMEM(padded, f32),
                pltpu.VMEM(big, f32),
                pltpu.VMEM(big, f32),
                pltpu.VMEM((depth + 1, 2 * rows, 2 * cols), f32),
                pltpu.VMEM(big, f32),
                pltpu.VMEM((6, depth, rows, cols), f32),
                pltpu.VMEM((2, face, cols), f32),
                pltpu.VMEM((2, face, cols), f32),
                pltpu.VMEM((6, rows, cols), f32),
                pltpu.VMEM((6, 6, rows, cols), f32),
                pltpu.VMEM((16, cols), f32),
                pltpu.VMEM((n_gx, 16, cols), f32),
                pltpu.VMEM((16, cols), f32),
                pltpu.VMEM((n_gy, 16, cols), f32),
                dma((8,)),
                dma((8,)),
                dma((n_gx,)),
                dma((n_gx,)),
                dma((n_gy,)),
                dma((n_gy,)),
            ],
            compiler_params=pltpu.CompilerParams(
                collective_id=0, has_side_effects=True, vmem_limit_bytes=32 * 1024 * 1024
            ),
        )(conductance, labels, cotangent, saved)

    return jax.shard_map(
        per_device,
        mesh=mesh,
        in_specs=(
            P(None, "gx", "gy"),
            P(None, "gx", "gy"),
            P(None, None, "gx", "gy"),
            P(None, None, "gx", "gy"),
        ),
        out_specs=(P(None, None, "gx", "gy"), P(None, "gx", "gy")),
        check_vma=False,
    )
```

time: 308 us -> 27.2 us (0.09)
  blocking collectives: 200 us -> 0 us
  waiting for transfers between devices: 55.4 us -> 0 us
  starting transfers between devices: 42.8 us -> 0 us
  Pallas kernels: 0 us -> 21.6 us
  other arithmetic: 4.61 us -> 0 us
  local copies, waits for them, and re-layouts: 0.82 us -> 4.77 us
    psum x5 -> x0, blocking collectives: 200 us -> none  [the longest x3 120 us: global_norm(): return lax.psum(class_sum(solver_residual, solver_residual), ('gx', 'gy'))]
    ppermute x20 -> x0, waiting for transfers between devices: 55.4 us -> none  [the longest x10 34.3 us: extended(): after = lax.ppermute(initial, axis, down)]
    ppermute x20 -> x0, starting transfers between devices: 42.8 us -> none  [the longest x10 29.8 us: extended(): before = lax.ppermute(last, axis, up)]
    pallas_call x0 -> x1, Pallas kernels: none -> 21.6 us  [per_device(): pl.pallas_call(lambda *refs: kernel(n_gx, n_gy, *refs), out_shape=(jax.Sh...]
    unnamed x10, local copies, waits for them, and re-layouts: 0.05 us -> 4.77 us
  transfers between devices with their start and end apart: 20 -> 0, of which waited for: 12 -> 0; matrix products, arithmetic and copies ran while one was open for 0% -> 0% of each run, Pallas kernels for 0% -> 0%
where the time goes in v1:
time: 27.2 us; the launch traced here: 27 us
  Pallas kernels  21.6 us (79%)
  local copies, waits for them, and re-layouts  4.77 us (18%)
  between operations  0.65 us (2%)
    pallas_call x1, Pallas kernels, per_device(): pl.pallas_call(lambda *refs: kernel(n_gx, n_gy, *refs), out_shape=(jax.Sh...  21.6 us
    unnamed x10, local copies, waits for them, and re-layouts  4.77 us

profile of v1, /device:TPU:0, one launch (start us, length us, event | category | flops | bytes accessed | tf_op | source)
XLA Modules:
  0.0 27.0 jit_solution(6254264961227973587)
XLA Ops:
  0.6 0.0 copy-start
  0.6 0.9 %copy-done = f32[2,16,8,128]{3,2,1,0:T(8,128)S(1)} copy-done((f32[2,16,8,128]{3,2,1,0:T(8,128)S(1)}, f32[2,16,8,128]{3,2,1,0:T(8,128)}, u32[]{:S(2)}) %copy-start) | copy-done | bytes 131096
  1.5 0.0 copy-start.1
  1.5 0.9 %copy-done.1 = f32[2,16,8,128]{3,2,1,0:T(8,128)S(1)} copy-done((f32[2,16,8,128]{3,2,1,0:T(8,128)S(1)}, f32[2,16,8,128]{3,2,1,0:T(8,128)}, u32[]{:S(2)}) %copy-start.1) | copy-done | bytes 131096
  2.4 0.0 copy-start.2
  2.4 0.8 %copy-done.2 = f32[16,8,128]{2,1,0:T(8,128)S(1)} copy-done((f32[16,8,128]{2,1,0:T(8,128)S(1)}, f32[16,8,128]{2,1,0:T(8,128)}, u32[]{:S(2)}) %copy-start.2) | copy-done | bytes 65560
  3.3 0.0 copy-start.3
  3.3 0.8 %copy-done.3 = s32[16,8,128]{2,1,0:T(8,128)S(1)} copy-done((s32[16,8,128]{2,1,0:T(8,128)S(1)}, s32[16,8,128]{2,1,0:T(8,128)}, u32[]{:S(2)}) %copy-start.3) | copy-done | bytes 65560
  4.1 21.6 %shard_map.59 = (f32[2,16,8,128]{3,2,1,0:T(8,128)S(1)}, f32[16,8,128]{2,1,0:T(8,128)S(1)}) custom-call(f32[16,8,128]{2,1,0:T(8,128)S(1)} %copy-done.2, s32[16,8,128]{2,1,0:T(8,128)S(1)} %copy-done.3, f32[2,16,8,128]{3,2,1,0:T(8,128)S(1)} %copy-done, f32[2,16,8,128]{3,2,1,0:T(8,128)S(1)} %copy-done.1), custom_call_target="tpu_custom_call" | custom-call | tf_op jit(solution)/shard_map/pallas_call | solution.py:345
  25.7 0.7 %copy.8 = f32[2,16,8,128]{3,2,1,0:T(8,128)} copy(f32[2,16,8,128]{3,2,1,0:T(8,128)S(1)} %get-tuple-element.4) | data formatting | bytes 262144
  26.4 0.6 %copy.9 = f32[16,8,128]{2,1,0:T(8,128)} copy(f32[16,8,128]{2,1,0:T(8,128)S(1)} %get-tuple-element.5) | data formatting | bytes 131072
Async XLA Ops:
  0.6 0.9 %copy-start = (f32[2,16,8,128]{3,2,1,0:T(8,128)S(1)}, f32[2,16,8,128]{3,2,1,0:T(8,128)}, u32[]{:S(2)}) copy-start(f32[2,16,8,128]{3,2,1,0:T(8,128)} %refs_2_.1) | copy-start | bytes 393220
  1.5 0.9 %copy-start.1 = (f32[2,16,8,128]{3,2,1,0:T(8,128)S(1)}, f32[2,16,8,128]{3,2,1,0:T(8,128)}, u32[]{:S(2)}) copy-start(f32[2,16,8,128]{3,2,1,0:T(8,128)} %refs_3_.1) | copy-start | bytes 393220
  2.4 0.8 %copy-start.2 = (f32[16,8,128]{2,1,0:T(8,128)S(1)}, f32[16,8,128]{2,1,0:T(8,128)}, u32[]{:S(2)}) copy-start(f32[16,8,128]{2,1,0:T(8,128)} %refs_0_.1) | copy-start | bytes 196612
  3.3 0.8 %copy-start.3 = (s32[16,8,128]{2,1,0:T(8,128)S(1)}, s32[16,8,128]{2,1,0:T(8,128)}, u32[]{:S(2)}) copy-start(s32[16,8,128]{2,1,0:T(8,128)} %refs_1_.1) | copy-start | bytes 196612

commit v2 on v1

--- a/solution.py
+++ b/solution.py
@@ -13,10 +13,11 @@
 
 def kernel(
     n_gx, n_gy,
-    cond_ref, label_ref, cot_ref, saved_ref,
+    cond_hbm, label_hbm, cot_hbm, saved_hbm,
     adj_ref, grad_ref,
+    cond_ref, label_ref, cot_ref, saved_ref, in_sem,
     ce, me, pe, v0, v1, v2, wx, wy, wz, dd, gk,
-    xsend, xrecv, ysend, yrecv, pay, slots_x, mid, slots_y,
+    xsend, xrecv, ysend, yrecv, table, pay, slots_x, mid, slots_y,
     send_sem, recv_sem, gx_send, gx_recv, gy_send, gy_recv,
 ):
     depth, rows, cols = cond_ref.shape
@@ -36,6 +37,15 @@
                 ok = here if ok is None else jnp.logical_and(ok, here)
         return ok
 
+    fetches = [
+        pltpu.make_async_copy(src, dst, in_sem.at[i])
+        for i, (src, dst) in enumerate((
+            (cond_hbm, cond_ref), (label_hbm, label_ref), (cot_hbm, cot_ref), (saved_hbm, saved_ref),
+        ))
+    ]
+    for fetch in fetches:
+        fetch.start()
+
     barrier = pltpu.get_barrier_semaphore()
     for o in range(1, n_gx):
         pl.semaphore_signal(barrier, inc=1, device_id=(lax.rem(gx + o, n_gx), gy), device_id_type=MESH)
@@ -46,10 +56,31 @@
         def _():
             pl.semaphore_signal(barrier, inc=1, device_id=(gx + dx, gy + dy), device_id_type=MESH)
 
+    zero_tile = jnp.zeros((rows, cols), jnp.float32)
+
+    edge = jnp.zeros((R2, C2), jnp.float32)
+    for v in (v0, v1, v2):
+        for k in range(2):
+            v[k, 0] = edge
+            v[k, depth + 1] = edge
+    wz[0] = edge
+    for z in range(depth):
+        for ref in (v0.at[0, z + 1], v0.at[1, z + 1], ce.at[z], me.at[z], pe.at[0, z], pe.at[1, z]):
+            ref[rows:R2, 0:cols] = zero_tile
+    for i, (dx, dy) in enumerate(sides):
+        @pl.when(jnp.logical_not(exists(dx, dy)))
+        def _():
+            if i < 2:
+                xrecv[i] = jnp.zeros(xrecv.shape[1:], jnp.float32)
+            else:
+                yrecv[i - 2] = jnp.zeros(yrecv.shape[1:], jnp.float32)
+
+    for fetch in fetches:
+        fetch.wait()
+
     lane = lax.broadcasted_iota(jnp.int32, (rows, cols), 1)
     slot_lanes = cols // depth
     packs = [jnp.zeros((rows, cols), jnp.float32) for _ in range(6)]
-    zero_tile = jnp.zeros((rows, cols), jnp.float32)
     for z in range(depth):
         lab = label_ref[z]
         m = jnp.where(lab == 0, 1.0, 0.0)
@@ -104,24 +135,7 @@
         def _():
             halo_copy(i).start()
 
-        @pl.when(jnp.logical_not(exists(dx, dy)))
-        def _():
-            if i < 2:
-                xrecv[i] = jnp.zeros(xrecv.shape[1:], jnp.float32)
-            else:
-                yrecv[i - 2] = jnp.zeros(yrecv.shape[1:], jnp.float32)
-
-    edge = jnp.zeros((R2, C2), jnp.float32)
-    for v in (v0, v1, v2):
-        for k in range(2):
-            v[k, 0] = edge
-            v[k, depth + 1] = edge
-    wz[0] = edge
-    for z in range(depth):
-        for ref in (v0.at[0, z + 1], v0.at[1, z + 1], ce.at[z], me.at[z], pe.at[0, z], pe.at[1, z]):
-            ref[rows:R2, 0:cols] = zero_tile
-
-    for i, (dx, dy) in enumerate(sides):
+    for i, (dx, dy) in enumerate(sides[2:], 2):
         @pl.when(exists(dx, dy))
         def _():
             arrival(i).wait_recv()
@@ -138,20 +152,30 @@
     window = jnp.logical_or(lane < HALO, lane >= cols - HALO)
     corner_rows = jnp.logical_or(row < HALO, row >= rows - HALO)
     window_corner = jnp.logical_and(window, corner_rows)
+    def targets(z):
+        return [v0.at[0, z + 1], v0.at[1, z + 1], ce.at[z], me.at[z], pe.at[0, z], pe.at[1, z]]
+
     for z in range(depth):
-        targets = [v0.at[0, z + 1], v0.at[1, z + 1], ce.at[z], me.at[z], pe.at[0, z], pe.at[1, z]]
-        at = 0
-        for f, (ref, width) in enumerate(zip(targets, (3, 3, 3, 2, 1, 1))):
-            first = at + z * width
-            ref[rows:rows + width, 0:cols] = xrecv[1, first:first + width, :]
-            ref[R2 - width:R2, 0:cols] = xrecv[0, first:first + width, :]
-            at += depth * width
+        for f, ref in enumerate(targets(z)):
             back = (cols - z * slot_lanes) % cols
             tile = pltpu.roll(beside[f], back, 1) if back else beside[f]
             ref[0:rows, cols:C2] = jnp.where(window, tile, 0.0)
             if f < 4:
                 tile = pltpu.roll(corner[f], back, 1) if back else corner[f]
                 ref[rows:R2, cols:C2] = jnp.where(window_corner, tile, 0.0)
+
+    for i, (dx, dy) in enumerate(sides[:2]):
+        @pl.when(exists(dx, dy))
+        def _():
+            arrival(i).wait_recv()
+
+    for z in range(depth):
+        at = 0
+        for ref, width in zip(targets(z), (3, 3, 3, 2, 1, 1)):
+            first = at + z * width
+            ref[rows:rows + width, 0:cols] = xrecv[1, first:first + width, :]
+            ref[R2 - width:R2, 0:cols] = xrecv[0, first:first + width, :]
+            at += depth * width
 
     big_row = lax.broadcasted_iota(jnp.int32, (R2, C2), 0)
     big_lane = lax.broadcasted_iota(jnp.int32, (R2, C2), 1)
@@ -188,7 +212,7 @@
         dd[z] = deg + (1.0 - SHIFT) / SCALE
         return carry
 
-    lax.fori_loop(0, depth, weights, 0, unroll=2)
+    lax.fori_loop(0, depth, weights, 0, unroll=depth)
 
     def apply_full(src, dst, sums):
         def body(z, carry):
@@ -206,7 +230,7 @@
                 out.append(carry[3 * k + 1] + old * new)
                 out.append(carry[3 * k + 2] + new * new)
             return tuple(out)
-        return lax.fori_loop(0, depth, body, (zero_tile,) * 6, unroll=2)
+        return lax.fori_loop(0, depth, body, (zero_tile,) * 6, unroll=depth)
 
     first = apply_full(v0, v1, True)
     second = apply_full(v1, v2, True)
@@ -227,14 +251,17 @@
             out.append(carry[k] + v * (m * a))
         return tuple(out)
 
-    third = lax.fori_loop(0, depth, apply_core, (zero_tile,) * 2, unroll=2)
+    third = lax.fori_loop(0, depth, apply_core, (zero_tile,) * 2, unroll=depth)
 
     for k in range(2):
         moments = [first[3 * k], first[3 * k + 1], first[3 * k + 2],
                    second[3 * k + 1], second[3 * k + 2], third[k]]
         for j, a in enumerate(moments):
-            pay[8 * k + j:8 * k + j + 1, :] = jnp.sum(a, axis=0, keepdims=True)
-        pay[8 * k + 6:8 * k + 8, :] = jnp.zeros((2, cols), jnp.float32)
+            table[8 * k + j:8 * k + j + 1, :] = jnp.sum(a, axis=0, keepdims=True)
+        table[8 * k + 6:8 * k + 8, :] = jnp.zeros((2, cols), jnp.float32)
+    diagonal = lax.broadcasted_iota(jnp.int32, (16, cols), 0) == lax.broadcasted_iota(jnp.int32, (16, cols), 1)
+    sums = jnp.broadcast_to(jnp.sum(table[...], axis=1, keepdims=True), (16, cols))
+    pay[...] = jnp.sum(jnp.where(diagonal, sums, 0.0), axis=0, keepdims=True)
 
     def gx_copy(o):
         return pltpu.make_async_remote_copy(
@@ -278,7 +305,7 @@
                 g = g + dn * (a - v[k, z, 0:rows, 0:cols])
                 gk[3 * k + j, z] = g
             return carry
-        lax.fori_loop(0, depth, body, 0, unroll=2)
+        lax.fori_loop(0, depth, body, 0, unroll=depth)
 
     parts(0)
     for o in range(1, n_gx):
@@ -296,7 +323,8 @@
     total = slots_y[0]
     for i in range(1, n_gy):
         total = total + slots_y[i]
-    total = jnp.broadcast_to(jnp.sum(total, axis=1, keepdims=True), total.shape)
+    total = jnp.where(diagonal, jnp.broadcast_to(total, (16, cols)), 0.0)
+    total = jnp.broadcast_to(jnp.sum(total, axis=1, keepdims=True), (16, cols))
 
     coeffs = []
     for k in range(2):
@@ -348,9 +376,14 @@
                 jax.ShapeDtypeStruct(cotangent.shape, f32),
                 jax.ShapeDtypeStruct(conductance.shape, f32),
             ),
-            in_specs=[vmem] * 4,
+            in_specs=[pl.BlockSpec(memory_space=pltpu.HBM)] * 4,
             out_specs=(vmem, vmem),
             scratch_shapes=[
+                pltpu.VMEM(conductance.shape, f32),
+                pltpu.VMEM(labels.shape, labels.dtype),
+                pltpu.VMEM(cotangent.shape, f32),
+                pltpu.VMEM(saved.shape, f32),
+                dma((4,)),
                 pltpu.VMEM(big, f32),
                 pltpu.VMEM(big, f32),
                 pltpu.VMEM((2,) + big, f32),
@@ -367,9 +400,10 @@
                 pltpu.VMEM((6, rows, cols), f32),
                 pltpu.VMEM((6, 6, rows, cols), f32),
                 pltpu.VMEM((16, cols), f32),
-                pltpu.VMEM((n_gx, 16, cols), f32),
-                pltpu.VMEM((16, cols), f32),
-                pltpu.VMEM((n_gy, 16, cols), f32),
+                pltpu.VMEM((1, cols), f32),
+                pltpu.VMEM((n_gx, 1, cols), f32),
+                pltpu.VMEM((1, cols), f32),
+                pltpu.VMEM((n_gy, 1, cols), f32),
                 dma((8,)),
                 dma((8,)),
                 dma((n_gx,)),

time: 27.2 us -> 25.3 us (0.930)
  Pallas kernels: 21.6 us -> 19.7 us
    pallas_call x1, Pallas kernels: 21.6 us -> 19.7 us  [per_device(): pl.pallas_call(lambda *refs: kernel(n_gx, n_gy, *refs), out_shape=(jax.Sh...]
where the time goes in v2:
time: 25.3 us; the launch traced here: 25.1 us
  Pallas kernels  19.7 us (78%)
  local copies, waits for them, and re-layouts  4.77 us (19%)
  between operations  0.65 us (3%)
    pallas_call x1, Pallas kernels, per_device(): pl.pallas_call(lambda *refs: kernel(n_gx, n_gy, *refs), out_shape=(jax.Sh...  19.7 us
    unnamed x10, local copies, waits for them, and re-layouts  4.77 us

profile of v2, /device:TPU:0, one launch (start us, length us, event | category | flops | bytes accessed | tf_op | source)
XLA Modules:
  0.0 25.1 jit_solution(16647073150357981413)
XLA Ops:
  0.6 0.0 copy-start
  0.6 0.9 %copy-done = f32[2,16,8,128]{3,2,1,0:T(8,128)S(1)} copy-done((f32[2,16,8,128]{3,2,1,0:T(8,128)S(1)}, f32[2,16,8,128]{3,2,1,0:T(8,128)}, u32[]{:S(2)}) %copy-start) | copy-done | bytes 131096
  1.5 0.0 copy-start.1
  1.5 0.9 %copy-done.1 = f32[2,16,8,128]{3,2,1,0:T(8,128)S(1)} copy-done((f32[2,16,8,128]{3,2,1,0:T(8,128)S(1)}, f32[2,16,8,128]{3,2,1,0:T(8,128)}, u32[]{:S(2)}) %copy-start.1) | copy-done | bytes 131096
  2.4 0.0 copy-start.2
  2.4 0.8 %copy-done.2 = f32[16,8,128]{2,1,0:T(8,128)S(1)} copy-done((f32[16,8,128]{2,1,0:T(8,128)S(1)}, f32[16,8,128]{2,1,0:T(8,128)}, u32[]{:S(2)}) %copy-start.2) | copy-done | bytes 65560
  3.3 0.0 copy-start.3
  3.3 0.8 %copy-done.3 = s32[16,8,128]{2,1,0:T(8,128)S(1)} copy-done((s32[16,8,128]{2,1,0:T(8,128)S(1)}, s32[16,8,128]{2,1,0:T(8,128)}, u32[]{:S(2)}) %copy-start.3) | copy-done | bytes 65560
  4.1 19.7 %shard_map.59 = (f32[2,16,8,128]{3,2,1,0:T(8,128)S(1)}, f32[16,8,128]{2,1,0:T(8,128)S(1)}) custom-call(f32[16,8,128]{2,1,0:T(8,128)S(1)} %copy-done.2, s32[16,8,128]{2,1,0:T(8,128)S(1)} %copy-done.3, f32[2,16,8,128]{3,2,1,0:T(8,128)S(1)} %copy-done, f32[2,16,8,128]{3,2,1,0:T(8,128)S(1)} %copy-done.1), custom_call_target="tpu_custom_call" | custom-call | tf_op jit(solution)/shard_map/pallas_call | solution.py:373
  23.8 0.7 %copy.8 = f32[2,16,8,128]{3,2,1,0:T(8,128)} copy(f32[2,16,8,128]{3,2,1,0:T(8,128)S(1)} %get-tuple-element.4) | data formatting | bytes 262144
  24.4 0.6 %copy.9 = f32[16,8,128]{2,1,0:T(8,128)} copy(f32[16,8,128]{2,1,0:T(8,128)S(1)} %get-tuple-element.5) | data formatting | bytes 131072
Async XLA Ops:
  0.6 0.9 %copy-start = (f32[2,16,8,128]{3,2,1,0:T(8,128)S(1)}, f32[2,16,8,128]{3,2,1,0:T(8,128)}, u32[]{:S(2)}) copy-start(f32[2,16,8,128]{3,2,1,0:T(8,128)} %refs_2_.1) | copy-start | bytes 393220
  1.5 0.9 %copy-start.1 = (f32[2,16,8,128]{3,2,1,0:T(8,128)S(1)}, f32[2,16,8,128]{3,2,1,0:T(8,128)}, u32[]{:S(2)}) copy-start(f32[2,16,8,128]{3,2,1,0:T(8,128)} %refs_3_.1) | copy-start | bytes 393220
  2.4 0.8 %copy-start.2 = (f32[16,8,128]{2,1,0:T(8,128)S(1)}, f32[16,8,128]{2,1,0:T(8,128)}, u32[]{:S(2)}) copy-start(f32[16,8,128]{2,1,0:T(8,128)} %refs_0_.1) | copy-start | bytes 196612
  3.3 0.8 %copy-start.3 = (s32[16,8,128]{2,1,0:T(8,128)S(1)}, s32[16,8,128]{2,1,0:T(8,128)}, u32[]{:S(2)}) copy-start(s32[16,8,128]{2,1,0:T(8,128)} %refs_1_.1) | copy-start | bytes 196612

commit v3 on v2

--- a/solution.py
+++ b/solution.py
@@ -17,8 +17,8 @@
     adj_ref, grad_ref,
     cond_ref, label_ref, cot_ref, saved_ref, in_sem,
     ce, me, pe, v0, v1, v2, wx, wy, wz, dd, gk,
-    xsend, xrecv, ysend, yrecv, table, pay, slots_x, mid, slots_y,
-    send_sem, recv_sem, gx_send, gx_recv, gy_send, gy_recv,
+    xsend, xrecv, ysend, yrecv, dsend, drecv, table, pay, slots,
+    send_sem, recv_sem, sum_send, sum_recv,
 ):
     depth, rows, cols = cond_ref.shape
     R2, C2 = 2 * rows, 2 * cols
@@ -36,6 +36,20 @@
                 here = low if d < 0 else high
                 ok = here if ok is None else jnp.logical_and(ok, here)
         return ok
+
+    count = n_gx * n_gy
+    own = gx * n_gy + gy
+
+    def peer(o):
+        other = lax.rem(own + o, count)
+        return lax.div(other, n_gy), lax.rem(other, n_gy)
+
+    def each_peer(act):
+        if count <= 64:
+            for o in range(1, count):
+                act(o)
+        else:
+            lax.fori_loop(1, count, lambda o, c: (act(o), c)[1], 0)
 
     fetches = [
         pltpu.make_async_copy(src, dst, in_sem.at[i])
@@ -47,14 +61,10 @@
         fetch.start()
 
     barrier = pltpu.get_barrier_semaphore()
-    for o in range(1, n_gx):
-        pl.semaphore_signal(barrier, inc=1, device_id=(lax.rem(gx + o, n_gx), gy), device_id_type=MESH)
-    for o in range(1, n_gy):
-        pl.semaphore_signal(barrier, inc=1, device_id=(gx, lax.rem(gy + o, n_gy)), device_id_type=MESH)
-    for dx, dy in sides[4:]:
-        @pl.when(exists(dx, dy))
-        def _():
-            pl.semaphore_signal(barrier, inc=1, device_id=(gx + dx, gy + dy), device_id_type=MESH)
+    def greet(o):
+        pl.semaphore_signal(barrier, inc=1, device_id=peer(o), device_id_type=MESH)
+
+    each_peer(greet)
 
     zero_tile = jnp.zeros((rows, cols), jnp.float32)
 
@@ -72,89 +82,101 @@
         def _():
             if i < 2:
                 xrecv[i] = jnp.zeros(xrecv.shape[1:], jnp.float32)
+            elif i < 4:
+                yrecv[i - 2] = jnp.zeros(yrecv.shape[1:], jnp.float32)
             else:
-                yrecv[i - 2] = jnp.zeros(yrecv.shape[1:], jnp.float32)
+                drecv[i - 4] = jnp.zeros(drecv.shape[1:], jnp.float32)
 
     for fetch in fetches:
         fetch.wait()
 
-    lane = lax.broadcasted_iota(jnp.int32, (rows, cols), 1)
-    slot_lanes = cols // depth
-    packs = [jnp.zeros((rows, cols), jnp.float32) for _ in range(6)]
+    def targets(z):
+        return [v0.at[0, z + 1], v0.at[1, z + 1], ce.at[z], me.at[z], pe.at[0, z], pe.at[1, z]]
+
     for z in range(depth):
         lab = label_ref[z]
         m = jnp.where(lab == 0, 1.0, 0.0)
         fields = [m * cot_ref[0, z], m * cot_ref[1, z], cond_ref[z], m]
         for k in range(2):
             fields.append(jnp.where(lab == k + 1, 1.0, jnp.where(lab > 0, 0.0, saved_ref[k, z])))
-        v0[0, z + 1, 0:rows, 0:cols] = fields[0]
-        v0[1, z + 1, 0:rows, 0:cols] = fields[1]
-        ce[z, 0:rows, 0:cols] = fields[2]
-        me[z, 0:rows, 0:cols] = m
-        pe[0, z, 0:rows, 0:cols] = fields[4]
-        pe[1, z, 0:rows, 0:cols] = fields[5]
         at = 0
-        for f, width in zip(fields, (3, 3, 3, 2, 1, 1)):
+        for f, ref, width in zip(fields, targets(z), (3, 3, 3, 2, 1, 1)):
+            ref[0:rows, 0:cols] = f
             first = at + z * width
             xsend[0, first:first + width, :] = f[0:width]
             xsend[1, first:first + width, :] = f[rows - width:rows]
             at += depth * width
-        window = lax.rem(lane - z * slot_lanes + HALO + cols, cols) < 2 * HALO
-        for i, f in enumerate(fields):
-            rolled = pltpu.roll(f, z * slot_lanes, 1) if z else f
-            packs[i] = jnp.where(window, rolled, packs[i])
-    for i in range(6):
-        ysend[i] = packs[i]
-
-    partners = n_gx - 1 + n_gy - 1
-    for dx, dy in sides[4:]:
-        partners = partners + jnp.where(exists(dx, dy), 1, 0)
-    pl.semaphore_wait(barrier, partners)
+
+    pl.semaphore_wait(barrier, count - 1)
 
     def halo_copy(i):
         dx, dy = sides[i]
         back = sides.index((-dx, -dy))
         if dy == 0:
             src, dst = xsend.at[0 if dx < 0 else 1], xrecv.at[back]
+        elif dx == 0:
+            src, dst = ysend, yrecv.at[back - 2]
         else:
-            src, dst = ysend, yrecv.at[back - 2]
+            src, dst = dsend.at[0 if dx < 0 else 1], drecv.at[back - 4]
         return pltpu.make_async_remote_copy(
             src_ref=src, dst_ref=dst, send_sem=send_sem.at[i], recv_sem=recv_sem.at[back],
             device_id=(gx + dx, gy + dy), device_id_type=MESH,
         )
 
     def arrival(i):
-        dst = xrecv.at[i] if i < 2 else yrecv.at[i - 2]
+        dst = xrecv.at[i] if i < 2 else yrecv.at[i - 2] if i < 4 else drecv.at[i - 4]
         return pltpu.make_async_remote_copy(
             src_ref=dst, dst_ref=dst, send_sem=send_sem.at[i], recv_sem=recv_sem.at[i],
             device_id=(gx + sides[i][0], gy + sides[i][1]), device_id_type=MESH,
         )
 
-    for i, (dx, dy) in enumerate(sides):
-        @pl.when(exists(dx, dy))
-        def _():
-            halo_copy(i).start()
-
-    for i, (dx, dy) in enumerate(sides[2:], 2):
-        @pl.when(exists(dx, dy))
-        def _():
-            arrival(i).wait_recv()
-
+    def send(first, end):
+        for i in range(first, end):
+            @pl.when(exists(*sides[i]))
+            def _():
+                halo_copy(i).start()
+
+    def receive(first, end):
+        for i in range(first, end):
+            @pl.when(exists(*sides[i]))
+            def _():
+                arrival(i).wait_recv()
+
+    send(0, 2)
+    lane = lax.broadcasted_iota(jnp.int32, (rows, cols), 1)
     row = lax.broadcasted_iota(jnp.int32, (rows, cols), 0)
+    slot_lanes = cols // depth
+    packs = [zero_tile] * 6
+    for z in range(depth):
+        window = lax.rem(lane - z * slot_lanes + HALO + cols, cols) < 2 * HALO
+        for i, ref in enumerate(targets(z)):
+            f = ref[0:rows, 0:cols]
+            rolled = pltpu.roll(f, z * slot_lanes, 1) if z else f
+            packs[i] = jnp.where(window, rolled, packs[i])
+    for i in range(6):
+        ysend[i] = packs[i]
+    send(2, 4)
+    for j in range(2):
+        one, other = packs[2 * j], packs[2 * j + 1]
+        dsend[0, j] = jnp.where(row < HALO, one, pltpu.roll(other, HALO, 0))
+        dsend[1, j] = jnp.where(row >= rows - HALO, one, pltpu.roll(other, rows - HALO, 0))
+    send(4, 8)
+
+    receive(2, 8)
     after = lax.rem(lane, slot_lanes) < HALO
     beside, corner = [], []
     for i in range(6):
         beside.append(jnp.where(after, yrecv[1, i], yrecv[0, i]))
         if i < 4:
-            above = jnp.where(after, yrecv[3, i], yrecv[2, i])
-            below = jnp.where(after, yrecv[5, i], yrecv[4, i])
+            above = jnp.where(after, drecv[1, i // 2], drecv[0, i // 2])
+            below = jnp.where(after, drecv[3, i // 2], drecv[2, i // 2])
+            if i % 2:
+                above = pltpu.roll(above, HALO, 0)
+                below = pltpu.roll(below, rows - HALO, 0)
             corner.append(jnp.where(row < rows // 2, below, above))
     window = jnp.logical_or(lane < HALO, lane >= cols - HALO)
     corner_rows = jnp.logical_or(row < HALO, row >= rows - HALO)
     window_corner = jnp.logical_and(window, corner_rows)
-    def targets(z):
-        return [v0.at[0, z + 1], v0.at[1, z + 1], ce.at[z], me.at[z], pe.at[0, z], pe.at[1, z]]
-
     for z in range(depth):
         for f, ref in enumerate(targets(z)):
             back = (cols - z * slot_lanes) % cols
@@ -164,10 +186,7 @@
                 tile = pltpu.roll(corner[f], back, 1) if back else corner[f]
                 ref[rows:R2, cols:C2] = jnp.where(window_corner, tile, 0.0)
 
-    for i, (dx, dy) in enumerate(sides[:2]):
-        @pl.when(exists(dx, dy))
-        def _():
-            arrival(i).wait_recv()
+    receive(0, 2)
 
     for z in range(depth):
         at = 0
@@ -263,21 +282,14 @@
     sums = jnp.broadcast_to(jnp.sum(table[...], axis=1, keepdims=True), (16, cols))
     pay[...] = jnp.sum(jnp.where(diagonal, sums, 0.0), axis=0, keepdims=True)
 
-    def gx_copy(o):
+    def sum_copy(o):
         return pltpu.make_async_remote_copy(
-            src_ref=pay, dst_ref=slots_x.at[gx], send_sem=gx_send.at[o], recv_sem=gx_recv.at[o],
-            device_id=(lax.rem(gx + o, n_gx), gy), device_id_type=MESH,
+            src_ref=pay, dst_ref=slots.at[own], send_sem=sum_send.at[o], recv_sem=sum_recv.at[o],
+            device_id=peer(o), device_id_type=MESH,
         )
 
-    def gy_copy(o):
-        return pltpu.make_async_remote_copy(
-            src_ref=mid, dst_ref=slots_y.at[gy], send_sem=gy_send.at[o], recv_sem=gy_recv.at[o],
-            device_id=(gx, lax.rem(gy + o, n_gy)), device_id_type=MESH,
-        )
-
-    for o in range(1, n_gx):
-        gx_copy(o).start()
-    slots_x[gx] = pay[...]
+    each_peer(lambda o: sum_copy(o).start())
+    slots[own] = pay[...]
 
     vx_edge = valid_x[:, 0:cols]
     vy_edge = valid_y[0:rows, :]
@@ -308,21 +320,9 @@
         lax.fori_loop(0, depth, body, 0, unroll=depth)
 
     parts(0)
-    for o in range(1, n_gx):
-        gx_copy(o).wait_recv()
-    total = slots_x[0]
-    for i in range(1, n_gx):
-        total = total + slots_x[i]
-    mid[...] = total
-    for o in range(1, n_gy):
-        gy_copy(o).start()
-    slots_y[gy] = total
     parts(1)
-    for o in range(1, n_gy):
-        gy_copy(o).wait_recv()
-    total = slots_y[0]
-    for i in range(1, n_gy):
-        total = total + slots_y[i]
+    each_peer(lambda o: sum_copy(o).wait_recv())
+    total = jnp.sum(slots[...], axis=0)
     total = jnp.where(diagonal, jnp.broadcast_to(total, (16, cols)), 0.0)
     total = jnp.broadcast_to(jnp.sum(total, axis=1, keepdims=True), (16, cols))
 
@@ -353,10 +353,7 @@
         @pl.when(exists(dx, dy))
         def _():
             halo_copy(i).wait_send()
-    for o in range(1, n_gx):
-        gx_copy(o).wait_send()
-    for o in range(1, n_gy):
-        gy_copy(o).wait_send()
+    each_peer(lambda o: sum_copy(o).wait_send())
 
 
 def solution(mesh):
@@ -398,18 +395,16 @@
                 pltpu.VMEM((2, face, cols), f32),
                 pltpu.VMEM((2, face, cols), f32),
                 pltpu.VMEM((6, rows, cols), f32),
-                pltpu.VMEM((6, 6, rows, cols), f32),
+                pltpu.VMEM((2, 6, rows, cols), f32),
+                pltpu.VMEM((2, 2, rows, cols), f32),
+                pltpu.VMEM((4, 2, rows, cols), f32),
                 pltpu.VMEM((16, cols), f32),
                 pltpu.VMEM((1, cols), f32),
-                pltpu.VMEM((n_gx, 1, cols), f32),
-                pltpu.VMEM((1, cols), f32),
-                pltpu.VMEM((n_gy, 1, cols), f32),
+                pltpu.VMEM((n_gx * n_gy, 1, cols), f32),
                 dma((8,)),
                 dma((8,)),
-                dma((n_gx,)),
-                dma((n_gx,)),
-                dma((n_gy,)),
-                dma((n_gy,)),
+                dma((n_gx * n_gy,)),
+                dma((n_gx * n_gy,)),
             ],
             compiler_params=pltpu.CompilerParams(
                 collective_id=0, has_side_effects=True, vmem_limit_bytes=32 * 1024 * 1024

time: 25.3 us -> 25.6 us (1.012)
  the two profiles are of different devices: /device:TPU:0 before, /device:TPU:1 now
where the time goes in v3:
time: 25.6 us; the launch traced here: 25.3 us
  Pallas kernels  19.9 us (78%)
  local copies, waits for them, and re-layouts  4.77 us (19%)
  between operations  0.65 us (3%)
    pallas_call x1, Pallas kernels, per_device(): pl.pallas_call(lambda *refs: kernel(n_gx, n_gy, *refs), out_shape=(jax.Sh...  19.9 us
    unnamed x10, local copies, waits for them, and re-layouts  4.77 us

profile of v3, /device:TPU:1, one launch (start us, length us, event | category | flops | bytes accessed | tf_op | source)
XLA Modules:
  0.0 25.3 jit_solution(13885263538303866204)
XLA Ops:
  0.6 0.0 copy-start
  0.6 0.9 %copy-done = f32[2,16,8,128]{3,2,1,0:T(8,128)S(1)} copy-done((f32[2,16,8,128]{3,2,1,0:T(8,128)S(1)}, f32[2,16,8,128]{3,2,1,0:T(8,128)}, u32[]{:S(2)}) %copy-start) | copy-done | bytes 131096
  1.5 0.0 copy-start.1
  1.5 0.9 %copy-done.1 = f32[2,16,8,128]{3,2,1,0:T(8,128)S(1)} copy-done((f32[2,16,8,128]{3,2,1,0:T(8,128)S(1)}, f32[2,16,8,128]{3,2,1,0:T(8,128)}, u32[]{:S(2)}) %copy-start.1) | copy-done | bytes 131096
  2.4 0.0 copy-start.2
  2.4 0.8 %copy-done.2 = f32[16,8,128]{2,1,0:T(8,128)S(1)} copy-done((f32[16,8,128]{2,1,0:T(8,128)S(1)}, f32[16,8,128]{2,1,0:T(8,128)}, u32[]{:S(2)}) %copy-start.2) | copy-done | bytes 65560
  3.3 0.0 copy-start.3
  3.3 0.8 %copy-done.3 = s32[16,8,128]{2,1,0:T(8,128)S(1)} copy-done((s32[16,8,128]{2,1,0:T(8,128)S(1)}, s32[16,8,128]{2,1,0:T(8,128)}, u32[]{:S(2)}) %copy-start.3) | copy-done | bytes 65560
  4.1 19.9 %shard_map.59 = (f32[2,16,8,128]{3,2,1,0:T(8,128)S(1)}, f32[16,8,128]{2,1,0:T(8,128)S(1)}) custom-call(f32[16,8,128]{2,1,0:T(8,128)S(1)} %copy-done.2, s32[16,8,128]{2,1,0:T(8,128)S(1)} %copy-done.3, f32[2,16,8,128]{3,2,1,0:T(8,128)S(1)} %copy-done, f32[2,16,8,128]{3,2,1,0:T(8,128)S(1)} %copy-done.1), custom_call_target="tpu_custom_call" | custom-call | tf_op jit(solution)/shard_map/pallas_call | solution.py:370
  24.0 0.7 %copy.8 = f32[2,16,8,128]{3,2,1,0:T(8,128)} copy(f32[2,16,8,128]{3,2,1,0:T(8,128)S(1)} %get-tuple-element.4) | data formatting | bytes 262144
  24.7 0.6 %copy.9 = f32[16,8,128]{2,1,0:T(8,128)} copy(f32[16,8,128]{2,1,0:T(8,128)S(1)} %get-tuple-element.5) | data formatting | bytes 131072
Async XLA Ops:
  0.6 0.9 %copy-start = (f32[2,16,8,128]{3,2,1,0:T(8,128)S(1)}, f32[2,16,8,128]{3,2,1,0:T(8,128)}, u32[]{:S(2)}) copy-start(f32[2,16,8,128]{3,2,1,0:T(8,128)} %refs_2_.1) | copy-start | bytes 393220
  1.5 0.9 %copy-start.1 = (f32[2,16,8,128]{3,2,1,0:T(8,128)S(1)}, f32[2,16,8,128]{3,2,1,0:T(8,128)}, u32[]{:S(2)}) copy-start(f32[2,16,8,128]{3,2,1,0:T(8,128)} %refs_3_.1) | copy-start | bytes 393220
  2.4 0.8 %copy-start.2 = (f32[16,8,128]{2,1,0:T(8,128)S(1)}, f32[16,8,128]{2,1,0:T(8,128)}, u32[]{:S(2)}) copy-start(f32[16,8,128]{2,1,0:T(8,128)} %refs_0_.1) | copy-start | bytes 196612
  3.3 0.8 %copy-start.3 = (s32[16,8,128]{2,1,0:T(8,128)S(1)}, s32[16,8,128]{2,1,0:T(8,128)}, u32[]{:S(2)}) copy-start(s32[16,8,128]{2,1,0:T(8,128)} %refs_1_.1) | copy-start | bytes 196612

commit v4 on v3

--- a/solution.py
+++ b/solution.py
@@ -17,8 +17,8 @@
     adj_ref, grad_ref,
     cond_ref, label_ref, cot_ref, saved_ref, in_sem,
     ce, me, pe, v0, v1, v2, wx, wy, wz, dd, gk,
-    xsend, xrecv, ysend, yrecv, dsend, drecv, table, pay, slots,
-    send_sem, recv_sem, sum_send, sum_recv,
+    xsend, xrecv, ysend, yrecv, dsend, drecv, table, pay, slots_x, mid, slots_y,
+    send_sem, recv_sem, gx_send, gx_recv, gy_send, gy_recv,
 ):
     depth, rows, cols = cond_ref.shape
     R2, C2 = 2 * rows, 2 * cols
@@ -36,20 +36,6 @@
                 here = low if d < 0 else high
                 ok = here if ok is None else jnp.logical_and(ok, here)
         return ok
-
-    count = n_gx * n_gy
-    own = gx * n_gy + gy
-
-    def peer(o):
-        other = lax.rem(own + o, count)
-        return lax.div(other, n_gy), lax.rem(other, n_gy)
-
-    def each_peer(act):
-        if count <= 64:
-            for o in range(1, count):
-                act(o)
-        else:
-            lax.fori_loop(1, count, lambda o, c: (act(o), c)[1], 0)
 
     fetches = [
         pltpu.make_async_copy(src, dst, in_sem.at[i])
@@ -61,10 +47,17 @@
         fetch.start()
 
     barrier = pltpu.get_barrier_semaphore()
-    def greet(o):
-        pl.semaphore_signal(barrier, inc=1, device_id=peer(o), device_id_type=MESH)
-
-    each_peer(greet)
+    partners = n_gx - 1 + n_gy - 1
+    for dx, dy in sides[4:]:
+        partners = partners + jnp.where(exists(dx, dy), 1, 0)
+
+        @pl.when(exists(dx, dy))
+        def _():
+            pl.semaphore_signal(barrier, inc=1, device_id=(gx + dx, gy + dy), device_id_type=MESH)
+    for o in range(1, n_gy):
+        pl.semaphore_signal(barrier, inc=1, device_id=(gx, lax.rem(gy + o, n_gy)), device_id_type=MESH)
+    for o in range(1, n_gx):
+        pl.semaphore_signal(barrier, inc=1, device_id=(lax.rem(gx + o, n_gx), gy), device_id_type=MESH)
 
     zero_tile = jnp.zeros((rows, cols), jnp.float32)
 
@@ -90,6 +83,8 @@
     for fetch in fetches:
         fetch.wait()
 
+    half = depth // 2
+
     def targets(z):
         return [v0.at[0, z + 1], v0.at[1, z + 1], ce.at[z], me.at[z], pe.at[0, z], pe.at[1, z]]
 
@@ -99,50 +94,48 @@
         fields = [m * cot_ref[0, z], m * cot_ref[1, z], cond_ref[z], m]
         for k in range(2):
             fields.append(jnp.where(lab == k + 1, 1.0, jnp.where(lab > 0, 0.0, saved_ref[k, z])))
-        at = 0
+        piece, at = z // half, 0
         for f, ref, width in zip(fields, targets(z), (3, 3, 3, 2, 1, 1)):
             ref[0:rows, 0:cols] = f
-            first = at + z * width
-            xsend[0, first:first + width, :] = f[0:width]
-            xsend[1, first:first + width, :] = f[rows - width:rows]
-            at += depth * width
-
-    pl.semaphore_wait(barrier, count - 1)
-
-    def halo_copy(i):
+            first = at + z % half * width
+            xsend[0, piece, first:first + width, :] = f[0:width]
+            xsend[1, piece, first:first + width, :] = f[rows - width:rows]
+            at += half * width
+
+    pl.semaphore_wait(barrier, partners)
+
+    def remote(i, src, dst, send_at, recv_at):
+        return pltpu.make_async_remote_copy(
+            src_ref=src, dst_ref=dst, send_sem=send_sem.at[send_at], recv_sem=recv_sem.at[recv_at],
+            device_id=(gx + sides[i][0], gy + sides[i][1]), device_id_type=MESH,
+        )
+
+    def halo_copies(i):
         dx, dy = sides[i]
         back = sides.index((-dx, -dy))
         if dy == 0:
-            src, dst = xsend.at[0 if dx < 0 else 1], xrecv.at[back]
-        elif dx == 0:
-            src, dst = ysend, yrecv.at[back - 2]
-        else:
-            src, dst = dsend.at[0 if dx < 0 else 1], drecv.at[back - 4]
-        return pltpu.make_async_remote_copy(
-            src_ref=src, dst_ref=dst, send_sem=send_sem.at[i], recv_sem=recv_sem.at[back],
-            device_id=(gx + dx, gy + dy), device_id_type=MESH,
-        )
-
-    def arrival(i):
-        dst = xrecv.at[i] if i < 2 else yrecv.at[i - 2] if i < 4 else drecv.at[i - 4]
-        return pltpu.make_async_remote_copy(
-            src_ref=dst, dst_ref=dst, send_sem=send_sem.at[i], recv_sem=recv_sem.at[i],
-            device_id=(gx + sides[i][0], gy + sides[i][1]), device_id_type=MESH,
-        )
-
-    def send(first, end):
+            return [
+                remote(i, xsend.at[i, p], xrecv.at[back, p], i + 8 * p, back + 8 * p) for p in range(2)
+            ]
+        if dx == 0:
+            return [remote(i, ysend, yrecv.at[back - 2], i, back)]
+        return [remote(i, dsend.at[0 if dx < 0 else 1], drecv.at[back - 4], i, back)]
+
+    def send(first, end, p=0):
         for i in range(first, end):
             @pl.when(exists(*sides[i]))
             def _():
-                halo_copy(i).start()
-
-    def receive(first, end):
+                halo_copies(i)[p].start()
+
+    def receive(first, end, p=0):
         for i in range(first, end):
             @pl.when(exists(*sides[i]))
             def _():
-                arrival(i).wait_recv()
+                dst = xrecv.at[i, p] if i < 2 else yrecv.at[i - 2] if i < 4 else drecv.at[i - 4]
+                remote(i, dst, dst, i + 8 * p, i + 8 * p).wait_recv()
 
     send(0, 2)
+    send(0, 2, 1)
     lane = lax.broadcasted_iota(jnp.int32, (rows, cols), 1)
     row = lax.broadcasted_iota(jnp.int32, (rows, cols), 0)
     slot_lanes = cols // depth
@@ -162,39 +155,42 @@
         dsend[1, j] = jnp.where(row >= rows - HALO, one, pltpu.roll(other, rows - HALO, 0))
     send(4, 8)
 
-    receive(2, 8)
+    receive(2, 4)
     after = lax.rem(lane, slot_lanes) < HALO
-    beside, corner = [], []
-    for i in range(6):
-        beside.append(jnp.where(after, yrecv[1, i], yrecv[0, i]))
-        if i < 4:
-            above = jnp.where(after, drecv[1, i // 2], drecv[0, i // 2])
-            below = jnp.where(after, drecv[3, i // 2], drecv[2, i // 2])
-            if i % 2:
-                above = pltpu.roll(above, HALO, 0)
-                below = pltpu.roll(below, rows - HALO, 0)
-            corner.append(jnp.where(row < rows // 2, below, above))
     window = jnp.logical_or(lane < HALO, lane >= cols - HALO)
     corner_rows = jnp.logical_or(row < HALO, row >= rows - HALO)
     window_corner = jnp.logical_and(window, corner_rows)
+
+    def unroll_lanes(tile, z):
+        back = (cols - z * slot_lanes) % cols
+        return pltpu.roll(tile, back, 1) if back else tile
+
+    beside = [jnp.where(after, yrecv[1, i], yrecv[0, i]) for i in range(6)]
     for z in range(depth):
         for f, ref in enumerate(targets(z)):
-            back = (cols - z * slot_lanes) % cols
-            tile = pltpu.roll(beside[f], back, 1) if back else beside[f]
-            ref[0:rows, cols:C2] = jnp.where(window, tile, 0.0)
-            if f < 4:
-                tile = pltpu.roll(corner[f], back, 1) if back else corner[f]
-                ref[rows:R2, cols:C2] = jnp.where(window_corner, tile, 0.0)
-
-    receive(0, 2)
-
-    for z in range(depth):
-        at = 0
-        for ref, width in zip(targets(z), (3, 3, 3, 2, 1, 1)):
-            first = at + z * width
-            ref[rows:rows + width, 0:cols] = xrecv[1, first:first + width, :]
-            ref[R2 - width:R2, 0:cols] = xrecv[0, first:first + width, :]
-            at += depth * width
+            ref[0:rows, cols:C2] = jnp.where(window, unroll_lanes(beside[f], z), 0.0)
+
+    receive(4, 8)
+    corner = []
+    for i in range(4):
+        above = jnp.where(after, drecv[1, i // 2], drecv[0, i // 2])
+        below = jnp.where(after, drecv[3, i // 2], drecv[2, i // 2])
+        if i % 2:
+            above = pltpu.roll(above, HALO, 0)
+            below = pltpu.roll(below, rows - HALO, 0)
+        corner.append(jnp.where(row < rows // 2, below, above))
+    for z in range(depth):
+        for f, ref in enumerate(targets(z)[:4]):
+            ref[rows:R2, cols:C2] = jnp.where(window_corner, unroll_lanes(corner[f], z), 0.0)
+
+    def unpack_x(p):
+        for z in range(half):
+            at = 0
+            for ref, width in zip(targets(p * half + z), (3, 3, 3, 2, 1, 1)):
+                first = at + z * width
+                ref[rows:rows + width, 0:cols] = xrecv[1, p, first:first + width, :]
+                ref[R2 - width:R2, 0:cols] = xrecv[0, p, first:first + width, :]
+                at += half * width
 
     big_row = lax.broadcasted_iota(jnp.int32, (R2, C2), 0)
     big_lane = lax.broadcasted_iota(jnp.int32, (R2, C2), 1)
@@ -231,9 +227,7 @@
         dd[z] = deg + (1.0 - SHIFT) / SCALE
         return carry
 
-    lax.fori_loop(0, depth, weights, 0, unroll=depth)
-
-    def apply_full(src, dst, sums):
+    def apply_full(src, dst, start, end, sums):
         def body(z, carry):
             ex, ey, ez, ezm, d, m = wx[z], wy[z], wz[z + 1], wz[z], dd[z], me[z]
             out = []
@@ -249,10 +243,18 @@
                 out.append(carry[3 * k + 1] + old * new)
                 out.append(carry[3 * k + 2] + new * new)
             return tuple(out)
-        return lax.fori_loop(0, depth, body, (zero_tile,) * 6, unroll=depth)
-
-    first = apply_full(v0, v1, True)
-    second = apply_full(v1, v2, True)
+        return lax.fori_loop(start, end, body, sums, unroll=end - start)
+
+    zero_sums = (zero_tile,) * 6
+    receive(0, 2)
+    unpack_x(0)
+    lax.fori_loop(0, half - 1, weights, 0, unroll=half - 1)
+    first = apply_full(v0, v1, 0, half - 1, zero_sums)
+    receive(0, 2, 1)
+    unpack_x(1)
+    lax.fori_loop(half - 1, depth, weights, 0, unroll=depth - half + 1)
+    first = apply_full(v0, v1, half - 1, depth, first)
+    second = apply_full(v1, v2, 0, depth, zero_sums)
 
     def apply_core(z, carry):
         exr = wx[z, :, 0:cols]
@@ -282,14 +284,21 @@
     sums = jnp.broadcast_to(jnp.sum(table[...], axis=1, keepdims=True), (16, cols))
     pay[...] = jnp.sum(jnp.where(diagonal, sums, 0.0), axis=0, keepdims=True)
 
-    def sum_copy(o):
+    def gx_copy(o):
         return pltpu.make_async_remote_copy(
-            src_ref=pay, dst_ref=slots.at[own], send_sem=sum_send.at[o], recv_sem=sum_recv.at[o],
-            device_id=peer(o), device_id_type=MESH,
+            src_ref=pay, dst_ref=slots_x.at[gx], send_sem=gx_send.at[o], recv_sem=gx_recv.at[o],
+            device_id=(lax.rem(gx + o, n_gx), gy), device_id_type=MESH,
         )
 
-    each_peer(lambda o: sum_copy(o).start())
-    slots[own] = pay[...]
+    def gy_copy(o):
+        return pltpu.make_async_remote_copy(
+            src_ref=mid, dst_ref=slots_y.at[gy], send_sem=gy_send.at[o], recv_sem=gy_recv.at[o],
+            device_id=(gx, lax.rem(gy + o, n_gy)), device_id_type=MESH,
+        )
+
+    for o in range(1, n_gx):
+        gx_copy(o).start()
+    slots_x[gx] = pay[...]
 
     vx_edge = valid_x[:, 0:cols]
     vy_edge = valid_y[0:rows, :]
@@ -320,9 +329,17 @@
         lax.fori_loop(0, depth, body, 0, unroll=depth)
 
     parts(0)
+    for o in range(1, n_gx):
+        gx_copy(o).wait_recv()
+    total = jnp.sum(slots_x[...], axis=0)
+    mid[...] = total
+    for o in range(1, n_gy):
+        gy_copy(o).start()
+    slots_y[gy] = total
     parts(1)
-    each_peer(lambda o: sum_copy(o).wait_recv())
-    total = jnp.sum(slots[...], axis=0)
+    for o in range(1, n_gy):
+        gy_copy(o).wait_recv()
+    total = jnp.sum(slots_y[...], axis=0)
     total = jnp.where(diagonal, jnp.broadcast_to(total, (16, cols)), 0.0)
     total = jnp.broadcast_to(jnp.sum(total, axis=1, keepdims=True), (16, cols))
 
@@ -352,8 +369,12 @@
     for i, (dx, dy) in enumerate(sides):
         @pl.when(exists(dx, dy))
         def _():
-            halo_copy(i).wait_send()
-    each_peer(lambda o: sum_copy(o).wait_send())
+            for copy in halo_copies(i):
+                copy.wait_send()
+    for o in range(1, n_gx):
+        gx_copy(o).wait_send()
+    for o in range(1, n_gy):
+        gy_copy(o).wait_send()
 
 
 def solution(mesh):
@@ -364,7 +385,7 @@
         f32 = jnp.float32
         big = (depth, 2 * rows, 2 * cols)
         padded = (2, depth + 2, 2 * rows, 2 * cols)
-        face = depth * 13
+        face = (2, 2, depth // 2 * 13, cols)
         vmem = pl.BlockSpec(memory_space=pltpu.VMEM)
         dma = pltpu.SemaphoreType.DMA
         return pl.pallas_call(
@@ -392,19 +413,23 @@
                 pltpu.VMEM((depth + 1, 2 * rows, 2 * cols), f32),
                 pltpu.VMEM(big, f32),
                 pltpu.VMEM((6, depth, rows, cols), f32),
-                pltpu.VMEM((2, face, cols), f32),
-                pltpu.VMEM((2, face, cols), f32),
+                pltpu.VMEM(face, f32),
+                pltpu.VMEM(face, f32),
                 pltpu.VMEM((6, rows, cols), f32),
                 pltpu.VMEM((2, 6, rows, cols), f32),
                 pltpu.VMEM((2, 2, rows, cols), f32),
                 pltpu.VMEM((4, 2, rows, cols), f32),
                 pltpu.VMEM((16, cols), f32),
                 pltpu.VMEM((1, cols), f32),
-                pltpu.VMEM((n_gx * n_gy, 1, cols), f32),
-                dma((8,)),
-                dma((8,)),
-                dma((n_gx * n_gy,)),
-                dma((n_gx * n_gy,)),
+                pltpu.VMEM((n_gx, 1, cols), f32),
+                pltpu.VMEM((1, cols), f32),
+                pltpu.VMEM((n_gy, 1, cols), f32),
+                dma((10,)),
+                dma((10,)),
+                dma((n_gx,)),
+                dma((n_gx,)),
+                dma((n_gy,)),
+                dma((n_gy,)),
             ],
             compiler_params=pltpu.CompilerParams(
                 collective_id=0, has_side_effects=True, vmem_limit_bytes=32 * 1024 * 1024

time: 25.6 us -> 23.9 us (0.934)
  the two profiles are of different devices: /device:TPU:1 before, /device:TPU:0 now
where the time goes in v4:
time: 23.9 us; the launch traced here: 23.6 us
  Pallas kernels  18.2 us (76%)
  local copies, waits for them, and re-layouts  4.77 us (20%)
  between operations  0.65 us (3%)
    pallas_call x1, Pallas kernels, per_device(): pl.pallas_call(lambda *refs: kernel(n_gx, n_gy, *refs), out_shape=(jax.Sh...  18.2 us
    unnamed x10, local copies, waits for them, and re-layouts  4.77 us

profile of v4, /device:TPU:0, one launch (start us, length us, event | category | flops | bytes accessed | tf_op | source)
XLA Modules:
  0.0 23.6 jit_solution(17751686478827100396)
XLA Ops:
  0.6 0.0 copy-start
  0.6 0.9 %copy-done = f32[2,16,8,128]{3,2,1,0:T(8,128)S(1)} copy-done((f32[2,16,8,128]{3,2,1,0:T(8,128)S(1)}, f32[2,16,8,128]{3,2,1,0:T(8,128)}, u32[]{:S(2)}) %copy-start) | copy-done | bytes 131096
  1.5 0.0 copy-start.1
  1.5 0.9 %copy-done.1 = f32[2,16,8,128]{3,2,1,0:T(8,128)S(1)} copy-done((f32[2,16,8,128]{3,2,1,0:T(8,128)S(1)}, f32[2,16,8,128]{3,2,1,0:T(8,128)}, u32[]{:S(2)}) %copy-start.1) | copy-done | bytes 131096
  2.4 0.0 copy-start.2
  2.4 0.8 %copy-done.2 = f32[16,8,128]{2,1,0:T(8,128)S(1)} copy-done((f32[16,8,128]{2,1,0:T(8,128)S(1)}, f32[16,8,128]{2,1,0:T(8,128)}, u32[]{:S(2)}) %copy-start.2) | copy-done | bytes 65560
  3.3 0.0 copy-start.3
  3.3 0.8 %copy-done.3 = s32[16,8,128]{2,1,0:T(8,128)S(1)} copy-done((s32[16,8,128]{2,1,0:T(8,128)S(1)}, s32[16,8,128]{2,1,0:T(8,128)}, u32[]{:S(2)}) %copy-start.3) | copy-done | bytes 65560
  4.1 18.2 %shard_map.59 = (f32[2,16,8,128]{3,2,1,0:T(8,128)S(1)}, f32[16,8,128]{2,1,0:T(8,128)S(1)}) custom-call(f32[16,8,128]{2,1,0:T(8,128)S(1)} %copy-done.2, s32[16,8,128]{2,1,0:T(8,128)S(1)} %copy-done.3, f32[2,16,8,128]{3,2,1,0:T(8,128)S(1)} %copy-done, f32[2,16,8,128]{3,2,1,0:T(8,128)S(1)} %copy-done.1), custom_call_target="tpu_custom_call" | custom-call | tf_op jit(solution)/shard_map/pallas_call | solution.py:391
  22.4 0.7 %copy.8 = f32[2,16,8,128]{3,2,1,0:T(8,128)} copy(f32[2,16,8,128]{3,2,1,0:T(8,128)S(1)} %get-tuple-element.4) | data formatting | bytes 262144
  23.0 0.6 %copy.9 = f32[16,8,128]{2,1,0:T(8,128)} copy(f32[16,8,128]{2,1,0:T(8,128)S(1)} %get-tuple-element.5) | data formatting | bytes 131072
Async XLA Ops:
  0.6 0.9 %copy-start = (f32[2,16,8,128]{3,2,1,0:T(8,128)S(1)}, f32[2,16,8,128]{3,2,1,0:T(8,128)}, u32[]{:S(2)}) copy-start(f32[2,16,8,128]{3,2,1,0:T(8,128)} %refs_2_.1) | copy-start | bytes 393220
  1.5 0.9 %copy-start.1 = (f32[2,16,8,128]{3,2,1,0:T(8,128)S(1)}, f32[2,16,8,128]{3,2,1,0:T(8,128)}, u32[]{:S(2)}) copy-start(f32[2,16,8,128]{3,2,1,0:T(8,128)} %refs_3_.1) | copy-start | bytes 393220
  2.4 0.8 %copy-start.2 = (f32[16,8,128]{2,1,0:T(8,128)S(1)}, f32[16,8,128]{2,1,0:T(8,128)}, u32[]{:S(2)}) copy-start(f32[16,8,128]{2,1,0:T(8,128)} %refs_0_.1) | copy-start | bytes 196612
  3.3 0.8 %copy-start.3 = (s32[16,8,128]{2,1,0:T(8,128)S(1)}, s32[16,8,128]{2,1,0:T(8,128)}, u32[]{:S(2)}) copy-start(s32[16,8,128]{2,1,0:T(8,128)} %refs_1_.1) | copy-start | bytes 196612

commit v5 on v4

--- a/solution.py
+++ b/solution.py
@@ -377,6 +377,17 @@
         gy_copy(o).wait_send()
 
 
+def write_out(adj_ref, grad_ref, adj_out, grad_out, sem):
+    copies = [
+        pltpu.make_async_copy(adj_ref, adj_out, sem.at[0]),
+        pltpu.make_async_copy(grad_ref, grad_out, sem.at[1]),
+    ]
+    for copy in copies:
+        copy.start()
+    for copy in copies:
+        copy.wait()
+
+
 def solution(mesh):
     n_gx, n_gy = mesh.shape["gx"], mesh.shape["gy"]
 
@@ -388,7 +399,7 @@
         face = (2, 2, depth // 2 * 13, cols)
         vmem = pl.BlockSpec(memory_space=pltpu.VMEM)
         dma = pltpu.SemaphoreType.DMA
-        return pl.pallas_call(
+        results = pl.pallas_call(
             lambda *refs: kernel(n_gx, n_gy, *refs),
             out_shape=(
                 jax.ShapeDtypeStruct(cotangent.shape, f32),
@@ -432,9 +443,18 @@
                 dma((n_gy,)),
             ],
             compiler_params=pltpu.CompilerParams(
-                collective_id=0, has_side_effects=True, vmem_limit_bytes=32 * 1024 * 1024
+                collective_id=0, has_side_effects=True, vmem_limit_bytes=63 * 1024 * 1024
             ),
         )(conductance, labels, cotangent, saved)
+        hbm = pl.BlockSpec(memory_space=pltpu.HBM)
+        return pl.pallas_call(
+            write_out,
+            out_shape=tuple(jax.ShapeDtypeStruct(r.shape, f32) for r in results),
+            in_specs=[hbm] * 2,
+            out_specs=(hbm, hbm),
+            scratch_shapes=[dma((2,))],
+            compiler_params=pltpu.CompilerParams(vmem_limit_bytes=63 * 1024 * 1024),
+        )(*results)
 
     return jax.shard_map(
         per_device,

time: 23.9 us -> 26.3 us (1.10)
  Pallas kernels: 18.2 us -> 25.5 us
  local copies, waits for them, and re-layouts: 4.77 us -> 0 us
    pallas_call x0 -> x1, Pallas kernels: none -> 7.08 us  [per_device(): pl.pallas_call(write_out, out_shape=tuple((jax.ShapeDtypeStruct(r.shape,...]
    unnamed x10 -> x0, local copies, waits for them, and re-layouts: 4.77 us -> none
where the time goes in v5:
time: 26.3 us; the launch traced here: 26.2 us
  Pallas kernels  25.5 us (97%)
  between operations  0.64 us (2%)
    pallas_call x1, Pallas kernels, per_device(): pl.pallas_call(lambda *refs: kernel(n_gx, n_gy, *refs), out_shape=(jax.Sh...  18.5 us
    pallas_call x1, Pallas kernels, per_device(): pl.pallas_call(write_out, out_shape=tuple((jax.ShapeDtypeStruct(r.shape,...  7.08 us

profile of v5, /device:TPU:0, one launch (start us, length us, event | category | flops | bytes accessed | tf_op | source)
XLA Modules:
  0.0 26.2 jit_solution(6004607745741413481)
XLA Ops:
  0.6 18.5 %shard_map.59 = (f32[2,16,8,128]{3,2,1,0:T(8,128)}, f32[16,8,128]{2,1,0:T(8,128)}) custom-call(f32[16,8,128]{2,1,0:T(8,128)} %refs_0_.1, s32[16,8,128]{2,1,0:T(8,128)} %refs_1_.1, f32[2,16,8,128]{3,2,1,0:T(8,128)} %refs_2_.1, f32[2,16,8,128]{3,2,1,0:T(8,128)} %refs_3_.1), custom_call_target="tpu_custom_call" | custom-call | tf_op jit(solution)/shard_map/pallas_call | solution.py:402
  19.1 7.1 %shard_map.60 = (f32[2,16,8,128]{3,2,1,0:T(8,128)}, f32[16,8,128]{2,1,0:T(8,128)}) custom-call(f32[2,16,8,128]{3,2,1,0:T(8,128)} %get-tuple-element.4.adj_ref, f32[16,8,128]{2,1,0:T(8,128)} %get-tuple-element.5.grad_ref), custom_call_target="tpu_custom_call" | custom-call | tf_op jit(solution)/shard_map/pallas_call | solution.py:450

commit v6 on v4

--- a/solution.py
+++ b/solution.py
@@ -432,7 +432,7 @@
                 dma((n_gy,)),
             ],
             compiler_params=pltpu.CompilerParams(
-                collective_id=0, has_side_effects=True, vmem_limit_bytes=32 * 1024 * 1024
+                collective_id=0, has_side_effects=True, vmem_limit_bytes=63 * 1024 * 1024
             ),
         )(conductance, labels, cotangent, saved)
 

time: 23.9 us -> 21.5 us (0.90)
  local copies, waits for them, and re-layouts: 4.77 us -> 2.23 us
  Pallas kernels: 18.2 us -> 18.5 us
    unnamed x10 -> x4, local copies, waits for them, and re-layouts: 4.77 us -> 2.23 us
where the time goes in v6:
time: 21.5 us; the launch traced here: 21.3 us
  Pallas kernels  18.5 us (86%)
  local copies, waits for them, and re-layouts  2.23 us (10%)
  between operations  0.65 us (3%)
    pallas_call x1, Pallas kernels, per_device(): pl.pallas_call(lambda *refs: kernel(n_gx, n_gy, *refs), out_shape=(jax.Sh...  18.5 us
    unnamed x4, local copies, waits for them, and re-layouts  2.23 us

profile of v6, /device:TPU:0, one launch (start us, length us, event | category | flops | bytes accessed | tf_op | source)
XLA Modules:
  0.0 21.3 jit_solution(13215439113769160093)
XLA Ops:
  0.6 18.5 %shard_map.59 = (f32[2,16,8,128]{3,2,1,0:T(8,128)}, f32[16,8,128]{2,1,0:T(8,128)}) custom-call(f32[16,8,128]{2,1,0:T(8,128)} %refs_0_.1, s32[16,8,128]{2,1,0:T(8,128)} %refs_1_.1, f32[2,16,8,128]{3,2,1,0:T(8,128)} %refs_2_.1, f32[2,16,8,128]{3,2,1,0:T(8,128)} %refs_3_.1), custom_call_target="tpu_custom_call" | custom-call | tf_op jit(solution)/shard_map/pallas_call | solution.py:391
  19.1 0.0 copy-start
  19.1 1.6 %copy.8 = f32[2,16,8,128]{3,2,1,0:T(8,128)} copy(f32[2,16,8,128]{3,2,1,0:T(8,128)} %get-tuple-element.4) | data formatting | bytes 262144
  20.7 0.0 copy-done
  20.7 0.6 %copy.9 = f32[16,8,128]{2,1,0:T(8,128)} copy(f32[16,8,128]{2,1,0:T(8,128)S(1)} %copy-done) | data formatting | bytes 131072
Async XLA Ops:
  19.1 1.6 %copy-start = (f32[16,8,128]{2,1,0:T(8,128)S(1)}, f32[16,8,128]{2,1,0:T(8,128)}, u32[]{:S(2)}) copy-start(f32[16,8,128]{2,1,0:T(8,128)} %get-tuple-element.5) | copy-start | bytes 196612
